TPU v7x, 128 devices: a whole 4x4x4 slice. The times are simulated.
128 devices in a mesh: dp: 64 (over y, z_hi, x, core), tensor: 2 (over z_lo).
Axes of the slice: x: 4, y: 4, z: 4 (z_hi: 2, z_lo: 2; z = z_hi * 2 + z_lo), core: 2. Of those that a mesh axis runs over, the one named last changes fastest.
Arguments:
- tokens: bfloat16 [64, 1024, 768], P('dp'), may hold values from -6 to 6
- segment_ids: int32 [64, 1024], P('dp'), may hold values from 0 to 2, never falling along the last dimension, each value on 1 to 512 neighbouring positions
- norm_gain: bfloat16 [768], replicated, may hold values from 0.25 to 1.75
- proj_main: bfloat16 [768, 2, 1536], P(None, None, 'tensor'), may hold values from -0.21875 to 0.21875
- proj_state: bfloat16 [768, 256], replicated, may hold values from -0.21875 to 0.21875
- proj_step: bfloat16 [768, 24], P(None, 'tensor'), may hold values from -0.21875 to 0.21875
- conv_main: float32 [4, 1536], P(None, 'tensor'), may hold values from -3 to 3
- conv_state: float32 [4, 256], replicated, may hold values from -3 to 3
- bias_main: float32 [1536], P('tensor'), may hold values from -0.5 to 0.5
- bias_state: float32 [256], replicated, may hold values from -0.5 to 0.5
- step_bias: float32 [24], P('tensor'), may hold values from -6 to -3
- log_rate: float32 [24], P('tensor'), may hold values from -1.5 to 1
- skip_gain: float32 [24], P('tensor'), may hold values from 0.5 to 1.5
- gate_gain: bfloat16 [1536], P('tensor'), may hold values from 0.25 to 1.75
- out_proj: bfloat16 [1536, 768], P('tensor'), may hold values from -0.15625 to 0.15625
- cotangent: bfloat16 [64, 1024, 768], P('dp'), may hold values from -6 to 6
Outputs:
- mixed: bfloat16 [64, 1024, 768], P('dp')
- grad_tokens: bfloat16 [64, 1024, 768], P('dp')
- grad_normgain: float32 [768], replicated
- grad_projmain: float32 [768, 2, 1536], P('dp', None, 'tensor')
- grad_projstate: float32 [768, 256], P('dp')
- grad_projstep: float32 [768, 24], P('dp', 'tensor')
- grad_convmain: float32 [4, 1536], P(None, 'tensor')
- grad_convstate: float32 [4, 256], replicated
- grad_biasmain: float32 [1536], P('tensor')
- grad_biasstate: float32 [256], replicated
- grad_stepbias: float32 [24], P('tensor')
- grad_lograte: float32 [24], P('tensor')
- grad_skipgain: float32 [24], P('tensor')
- grad_gategain: float32 [1536], P('tensor')
- grad_outproj: float32 [1536, 768], P('tensor', 'dp')
Inputs may be any that keep to these rules, and one draw needn't show every extreme that they name: `segment_ids`: in each packed row the sequence numbers start at 0, never fall, and each of the 3 sequences covers 1 to 512 consecutive tokens.
All inputs are finite; a program needn't handle non-finite values.
Results may differ from a plain program's by a relative error of at most 0.012.
Values sent between devices are 32-bit elements; how exact they have to be, the bound alone decides.
No kernel may reach another device: no remote copies, remote signals or barrier semaphores. Data moves between devices by JAX's collectives and lax.ppermute only.
A program may use at most 192 MiB of HBM per device.

v0:
```python
import jax
import jax.numpy as jnp
from jax import lax
from jax.sharding import PartitionSpec as P

INNER = 1536
GROUP = 256


epsilon = 1e-05


def conv_masks(segment, taps):
    length = segment.shape[0]
    padded = jnp.concatenate([jnp.full((taps - 1,), -1, jnp.int32), segment])
    return [
        (padded[taps - 1 - offset : taps - 1 - offset + length] == segment).astype(jnp.float32)
        for offset in range(taps)
    ]


def causal_conv(values, kernel, shift, masks):
    taps = kernel.shape[0]
    length = values.shape[0]
    padded = jnp.pad(values, ((taps - 1, 0), (0, 0)))
    total = jnp.zeros_like(values) + shift[None, :]
    for offset in range(taps):
        moved = padded[taps - 1 - offset : taps - 1 - offset + length]
        total = total + moved * kernel[taps - 1 - offset][None, :] * masks[offset][:, None]
    return total


def ssd_block(carry, block):
    states, prior_id = carry
    values, step_sizes, log_decay, write_map, read_map, segment = block
    size = segment.shape[0]
    cumlog = jnp.cumsum(log_decay, axis=0)
    places = jnp.arange(size)
    same = (segment[:, None] == segment[None, :]) & (places[:, None] >= places[None, :])
    spread = cumlog[:, None, :] - cumlog[None, :, :]
    decay = jnp.exp(jnp.where(same[:, :, None], spread, 0.0)) * same.astype(jnp.float32)[:, :, None]
    intersection = jnp.dot(
        read_map, write_map.T, precision=lax.Precision.HIGHEST, preferred_element_type=jnp.float32
    )
    weights = decay * intersection[:, :, None] * step_sizes[None, :, :]
    inside = jnp.einsum("tsh,shp->thp", weights, values, precision=lax.Precision.HIGHEST)
    entry_scale = (segment == prior_id).astype(jnp.float32)[:, None] * jnp.exp(cumlog)
    across = (
        jnp.einsum("tn,hpn->thp", read_map, states, precision=lax.Precision.HIGHEST)
        * entry_scale[:, :, None]
    )
    tail_log = cumlog[size - 1]
    last_id = segment[size - 1]
    weight_back = (
        (segment == last_id).astype(jnp.float32)[:, None]
        * jnp.exp(tail_log[None, :] - cumlog)
        * step_sizes
    )
    carry_scale = (jnp.exp(tail_log) * (last_id == prior_id).astype(jnp.float32))[:, None, None]
    updates = jnp.einsum(
        "sh,shp,sn->hpn", weight_back, values, write_map, precision=lax.Precision.HIGHEST
    )
    return ((states * carry_scale + updates, last_id), inside + across)


def state_scan(values, step_sizes, log_decay, write_map, read_map, segment):
    length, head_count, head_dim = values.shape
    block = min(GROUP, length)
    blocks_count = length // block

    def split(member):
        return member.reshape((blocks_count, block) + member.shape[1:])

    start = (jnp.zeros((head_count, head_dim, write_map.shape[1]), jnp.float32), jnp.int32(-1))
    pieces = tuple(
        (split(member) for member in (values, step_sizes, log_decay, write_map, read_map, segment))
    )
    finished, outputs = lax.scan(jax.checkpoint(ssd_block), start, pieces)
    return outputs.reshape(length, head_count, head_dim)


def mixer(raw_main, state_mix, raw_step, weights, segment):
    conv_kernel, conv_shift, bias_step, rate_log, skip_weight = weights
    length = raw_main.shape[0]
    half_width = raw_main.shape[1] // 2
    gate_in = raw_main[:, :half_width]
    masks = conv_masks(segment, conv_kernel.shape[0])
    main_in = jax.nn.silu(causal_conv(raw_main[:, half_width:], conv_kernel, conv_shift, masks))
    state_width = state_mix.shape[1] // 2
    step_sizes = jax.nn.softplus(raw_step + bias_step[None, :])
    log_decay = -step_sizes * jnp.exp(rate_log)[None, :]
    head_count = bias_step.shape[0]
    values = main_in.reshape(length, head_count, half_width // head_count)
    scanned = state_scan(
        values,
        step_sizes,
        log_decay,
        state_mix[:, :state_width],
        state_mix[:, state_width:],
        segment,
    )
    output = scanned + skip_weight[None, :, None] * values
    return output.reshape(length, half_width) * jax.nn.silu(gate_in)


def state_conv(values, kernel, shift, segment):
    return jax.nn.silu(causal_conv(values, kernel, shift, conv_masks(segment, kernel.shape[0])))


def input_norm(values, gains):
    square = jnp.mean(values * values, axis=1, keepdims=True)
    return values * lax.rsqrt(square + epsilon) * gains[None, :]


def contract_rows(left, right):
    return lax.dot_general(
        left, right, (((0,), (0,)), ((), ())), preferred_element_type=jnp.float32
    )


def contract_cols(left, right):
    return lax.dot_general(
        left, right, (((1,), (1,)), ((), ())), preferred_element_type=jnp.float32
    )


def local(
    tokens,
    segment_ids,
    norm_gain,
    proj_main,
    proj_state,
    proj_step,
    conv_main,
    conv_state,
    bias_main,
    bias_state,
    step_bias,
    log_rate,
    skip_gain,
    gate_gain,
    out_proj,
    cotangent,
):
    packs, length, width = tokens.shape
    main_local = proj_main.shape[2]
    state_cols = proj_state.shape[1]
    step_cols = proj_step.shape[1]
    row_count = packs * length
    data = tokens.astype(jnp.float32).reshape(row_count, width)
    normed_full, norm_pull = jax.vjp(input_norm, data, norm_gain.astype(jnp.float32))
    normed = normed_full.astype(jnp.bfloat16)
    main_weight = proj_main.reshape(width, 2 * main_local)
    main_raw = jnp.dot(normed, main_weight, preferred_element_type=jnp.float32)
    state_raw = jnp.dot(normed, proj_state, preferred_element_type=jnp.float32)
    step_raw = jnp.dot(normed, proj_step, preferred_element_type=jnp.float32)

    def state_branch(values, kernel, shift):
        return jax.vmap(state_conv, in_axes=(0, None, None, 0))(values, kernel, shift, segment_ids)

    state_mix, state_pull = jax.vjp(
        state_branch, state_raw.reshape(packs, length, state_cols), conv_state, bias_state
    )
    params = tuple((member for member in (conv_main, bias_main, step_bias, log_rate, skip_gain)))

    def main_branch(raw_main, mix_state, raw_step, weights):
        return jax.vmap(mixer, in_axes=(0, 0, 0, None, 0))(
            raw_main, mix_state, raw_step, weights, segment_ids
        )

    gated_rows, main_pull = jax.vjp(
        main_branch,
        main_raw.reshape(packs, length, 2 * main_local),
        state_mix,
        step_raw.reshape(packs, length, step_cols),
        params,
    )
    gated = gated_rows.reshape(row_count, main_local)
    gains = gate_gain.astype(jnp.float32)
    local_squares = jnp.sum(gated * gated, axis=1)
    scaled = (gated * gains[None, :]).astype(jnp.bfloat16)
    local_part = jnp.dot(scaled, out_proj, preferred_element_type=jnp.float32)
    total_squares = lax.psum(local_squares, "tensor")
    rscale = lax.rsqrt(total_squares / INNER + epsilon)[:, None]
    out_branch = lax.psum(rscale * local_part, "tensor")
    mixed = (data + out_branch).astype(jnp.bfloat16).reshape(packs, length, width)
    grad_out = cotangent.astype(jnp.float32).reshape(row_count, width)
    grad_part = (rscale * grad_out).astype(jnp.bfloat16)
    grad_ratio = jnp.sum(grad_out * out_branch, axis=1, keepdims=True) * rscale * rscale
    outproj_local = contract_rows(scaled, grad_part)
    grad_scaled = contract_cols(grad_part, out_proj)
    gategain_local = jnp.sum(grad_scaled * gated, axis=0)
    grad_gated = grad_scaled * gains[None, :] - grad_ratio * gated / INNER
    grad_main, grad_mix, grad_steps, grad_params = main_pull(
        grad_gated.reshape(packs, length, main_local)
    )
    main_back = grad_main.reshape(row_count, 2 * main_local).astype(jnp.bfloat16)
    step_back = grad_steps.reshape(row_count, step_cols).astype(jnp.bfloat16)
    input_part = contract_cols(main_back, main_weight) + contract_cols(step_back, proj_step)
    input_sum, mix_sum = lax.psum((input_part, grad_mix.reshape(row_count, state_cols)), "tensor")
    grad_stateraw, convstate_local, biasstate_local = state_pull(
        mix_sum.reshape(packs, length, state_cols)
    )
    state_back = grad_stateraw.reshape(row_count, state_cols).astype(jnp.bfloat16)
    input_grad = input_sum + contract_cols(state_back, proj_state)
    grad_data, normgain_local = norm_pull(input_grad)
    grad_tokens = (grad_out + grad_data).astype(jnp.bfloat16).reshape(packs, length, width)
    joined = jnp.concatenate([main_back, state_back, step_back], axis=1)
    share = width // lax.axis_size("dp")
    reduced = lax.psum_scatter(contract_rows(normed, joined), "dp", scatter_dimension=0, tiled=True)
    grad_projmain = reduced[:, : 2 * main_local].reshape(share, 2, main_local)
    grad_projstate = reduced[:, 2 * main_local : 2 * main_local + state_cols]
    grad_projstep = reduced[:, 2 * main_local + state_cols :]
    grad_outproj = lax.psum_scatter(outproj_local, "dp", scatter_dimension=1, tiled=True)
    summed = lax.psum(
        (
            normgain_local,
            grad_params[0],
            grad_params[1],
            convstate_local,
            biasstate_local,
            grad_params[2],
            grad_params[3],
            grad_params[4],
            gategain_local,
        ),
        "dp",
    )
    return (
        mixed,
        grad_tokens,
        summed[0],
        grad_projmain,
        grad_projstate,
        grad_projstep,
        summed[1],
        summed[3],
        summed[2],
        summed[4],
        summed[5],
        summed[6],
        summed[7],
        summed[8],
        grad_outproj,
    )


def solution(mesh):
    placed = (
        P("dp", None, None),
        P("dp", None),
        P(),
        P(None, None, "tensor"),
        P(),
        P(None, "tensor"),
        P(None, "tensor"),
        P(),
        P("tensor"),
        P(),
        P("tensor"),
        P("tensor"),
        P("tensor"),
        P("tensor"),
        P("tensor", None),
        P("dp", None, None),
    )
    return jax.shard_map(
        local,
        mesh=mesh,
        in_specs=placed,
        out_specs=(
            P("dp", None, None),
            P("dp", None, None),
            P(),
            P("dp", None, "tensor"),
            P("dp", None),
            P("dp", "tensor"),
            P(None, "tensor"),
            P(),
            P("tensor"),
            P(),
            P("tensor"),
            P("tensor"),
            P("tensor"),
            P("tensor"),
            P("tensor", "dp"),
        ),
        check_vma=False,
    )
```

profile of v0, /device:TPU:0, one launch (start us, length us, event | category | flops | bytes accessed | tf_op | source)
XLA Modules:
  0.0 1423.1 jit_solution(5712961531647109642)
XLA Ops:
  29.6 4.4 fusion.161
  37.4 5.2 reshape.1397
  42.6 4.1 copy.254
  49.1 141.3 %while.45 = (s32[]{:T(128)}, f32[1,12,64,128]{3,2,1,0:T(8,128)S(1)}, s32[1]{0:T(128)}, f32[4,1,256,12,64]{2,0,4,3,1:T(4,128)}, f32[4,1,12,64,128]{4,3,2,1,0:T(8,...) while((s32[]{:T(128)}, ...), condition=%wide.region_4.5_spmd.clone, body=%wide.region_1.4_spmd.clone.sunk | while | flops 1314305024 | bytes 11143086 | solution.py:78
  57.3 5.0 fusion.270
  66.0 17.9 %dynamic_update_slice.86 = f32[4,1,256,12,64]{2,0,4,3,1:T(4,128)} dynamic-update-slice(f32[4,1,256,12,64]{2,0,4,3,1:T(4,128)} %get-tuple-element.1178, f32[1,1,256,12,64]{2,0,4,3,1:T(1,128)S(1)} %copy.377, s32[]{:T(128)S(6)} %copy.411, s32[]{:T(128)} %constant.132.clone.1..sunk, s32[]{:T(128)} %constant.132.clone.1..sunk, s32[]{:T(128)} %constant.132.clone.1..sunk, s32[]{:T(128)} %constant.132.clone.1..sunk) | dynamic-update-slice | bytes 1572868 | tf_op jit(solution)/shard_map/jvp(vmap())/while/body/jit(dynamic_update_index_in_dim)/dynamic_update_slice | solution.py:78
  92.5 5.0 fusion.270
  101.3 17.9 %dynamic_update_slice.86 = f32[4,1,256,12,64]{2,0,4,3,1:T(4,128)} dynamic-update-slice(f32[4,1,256,12,64]{2,0,4,3,1:T(4,128)} %get-tuple-element.1178, f32[1,1,256,12,64]{2,0,4,3,1:T(1,128)S(1)} %copy.377, s32[]{:T(128)S(6)} %copy.411, s32[]{:T(128)} %constant.132.clone.1..sunk, s32[]{:T(128)} %constant.132.clone.1..sunk, s32[]{:T(128)} %constant.132.clone.1..sunk, s32[]{:T(128)} %constant.132.clone.1..sunk) | dynamic-update-slice | bytes 1572868 | tf_op jit(solution)/shard_map/jvp(vmap())/while/body/jit(dynamic_update_index_in_dim)/dynamic_update_slice | solution.py:78
  127.8 5.0 fusion.270
  136.5 17.9 %dynamic_update_slice.86 = f32[4,1,256,12,64]{2,0,4,3,1:T(4,128)} dynamic-update-slice(f32[4,1,256,12,64]{2,0,4,3,1:T(4,128)} %get-tuple-element.1178, f32[1,1,256,12,64]{2,0,4,3,1:T(1,128)S(1)} %copy.377, s32[]{:T(128)S(6)} %copy.411, s32[]{:T(128)} %constant.132.clone.1..sunk, s32[]{:T(128)} %constant.132.clone.1..sunk, s32[]{:T(128)} %constant.132.clone.1..sunk, s32[]{:T(128)} %constant.132.clone.1..sunk) | dynamic-update-slice | bytes 1572868 | tf_op jit(solution)/shard_map/jvp(vmap())/while/body/jit(dynamic_update_index_in_dim)/dynamic_update_slice | solution.py:78
  163.1 5.0 fusion.270
  171.8 17.9 %dynamic_update_slice.86 = f32[4,1,256,12,64]{2,0,4,3,1:T(4,128)} dynamic-update-slice(f32[4,1,256,12,64]{2,0,4,3,1:T(4,128)} %get-tuple-element.1178, f32[1,1,256,12,64]{2,0,4,3,1:T(1,128)S(1)} %copy.377, s32[]{:T(128)S(6)} %copy.411, s32[]{:T(128)} %constant.132.clone.1..sunk, s32[]{:T(128)} %constant.132.clone.1..sunk, s32[]{:T(128)} %constant.132.clone.1..sunk, s32[]{:T(128)} %constant.132.clone.1..sunk) | dynamic-update-slice | bytes 1572868 | tf_op jit(solution)/shard_map/jvp(vmap())/while/body/jit(dynamic_update_index_in_dim)/dynamic_update_slice | solution.py:78
  190.4 5.2 transpose.175
  199.1 5.8 fusion.155
  204.9 4.9 psum.91
  209.9 5.0 convolution_multiply_fusion.1
  214.9 4.4 copy.336
  219.3 3.6 copy.270
  222.9 87.1 %all-reduce.33.cloned.1.call-done = f32[1024,768]{1,0:T(8,128)} async-done(((f32[1024,768]{1,0:T(8,128)}), f32[1024,768]{1,0:T(8,128)}) %all-reduce.33.cloned.1.call-update) | async-done | bytes 3145744 | tf_op jit(solution)/shard_map/psum | solution.py:185
  310.0 4.2 fusion.145
  315.3 8.6 multiply_reduce_fusion.2
  327.5 5.2 reshape.1405
  338.2 259.5 %while.46 = (s32[]{:T(128)}, f32[1,12,64,128]{3,2,1,0:T(8,128)S(1)}, f32[4,1,256,12,64]{2,0,4,3,1:T(4,128)}, f32[4,1,256,12]{3,2,1,0:T(8,128)}, f32[4,1,256,12]{...) while((s32[]{:T(128)}, ...), condition=%wide.region_21.22_spmd.clone, body=%wide.region_9.21_spmd.clone.sunk | while | flops 3038996480 | bytes 33094308 | solution.py:78
  364.2 5.1 fusion.291
  379.1 5.0 fusion.294
  392.8 17.9 %dynamic_update_slice.91 = f32[4,1,256,12,64]{2,0,4,3,1:T(4,128)} dynamic-update-slice(f32[4,1,256,12,64]{2,0,4,3,1:T(4,128)} %get-tuple-element.1227, f32[1,1,256,12,64]{2,0,4,3,1:T(1,128)S(1)} %copy.391, s32[]{:T(128)S(6)} %sub.327, s32[]{:T(128)} %constant.132.clone.1..sunk.1, s32[]{:T(128)} %constant.132.clone.1..sunk.1, s32[]{:T(128)} %constant.132.clone.1..sunk.1, s32[]{:T(128)} %constant.132.clone.1..sunk.1) | dynamic-update-slice | bytes 1572868 | tf_op jit(solution)/shard_map/transpose(jvp(vmap()))/while/body/jit(dynamic_update_index_in_dim)/dynamic_update_slice | solution.py:78
  426.5 5.1 fusion.291
  441.4 5.0 fusion.294
  455.1 17.9 %dynamic_update_slice.91 = f32[4,1,256,12,64]{2,0,4,3,1:T(4,128)} dynamic-update-slice(f32[4,1,256,12,64]{2,0,4,3,1:T(4,128)} %get-tuple-element.1227, f32[1,1,256,12,64]{2,0,4,3,1:T(1,128)S(1)} %copy.391, s32[]{:T(128)S(6)} %sub.327, s32[]{:T(128)} %constant.132.clone.1..sunk.1, s32[]{:T(128)} %constant.132.clone.1..sunk.1, s32[]{:T(128)} %constant.132.clone.1..sunk.1, s32[]{:T(128)} %constant.132.clone.1..sunk.1) | dynamic-update-slice | bytes 1572868 | tf_op jit(solution)/shard_map/transpose(jvp(vmap()))/while/body/jit(dynamic_update_index_in_dim)/dynamic_update_slice | solution.py:78
  488.8 5.1 fusion.291
  503.7 5.0 fusion.294
  517.4 17.9 %dynamic_update_slice.91 = f32[4,1,256,12,64]{2,0,4,3,1:T(4,128)} dynamic-update-slice(f32[4,1,256,12,64]{2,0,4,3,1:T(4,128)} %get-tuple-element.1227, f32[1,1,256,12,64]{2,0,4,3,1:T(1,128)S(1)} %copy.391, s32[]{:T(128)S(6)} %sub.327, s32[]{:T(128)} %constant.132.clone.1..sunk.1, s32[]{:T(128)} %constant.132.clone.1..sunk.1, s32[]{:T(128)} %constant.132.clone.1..sunk.1, s32[]{:T(128)} %constant.132.clone.1..sunk.1) | dynamic-update-slice | bytes 1572868 | tf_op jit(solution)/shard_map/transpose(jvp(vmap()))/while/body/jit(dynamic_update_index_in_dim)/dynamic_update_slice | solution.py:78
  551.1 5.1 fusion.291
  565.9 5.0 fusion.294
  579.7 17.9 %dynamic_update_slice.91 = f32[4,1,256,12,64]{2,0,4,3,1:T(4,128)} dynamic-update-slice(f32[4,1,256,12,64]{2,0,4,3,1:T(4,128)} %get-tuple-element.1227, f32[1,1,256,12,64]{2,0,4,3,1:T(1,128)S(1)} %copy.391, s32[]{:T(128)S(6)} %sub.327, s32[]{:T(128)} %constant.132.clone.1..sunk.1, s32[]{:T(128)} %constant.132.clone.1..sunk.1, s32[]{:T(128)} %constant.132.clone.1..sunk.1, s32[]{:T(128)} %constant.132.clone.1..sunk.1) | dynamic-update-slice | bytes 1572868 | tf_op jit(solution)/shard_map/transpose(jvp(vmap()))/while/body/jit(dynamic_update_index_in_dim)/dynamic_update_slice | solution.py:78
  599.9 5.3 transpose.176
  608.7 10.0 multiply_reduce_fusion.6
  630.5 115.8 %all-reduce.37.cloned.1.call-done = (f32[1024,768]{1,0:T(8,128)}, f32[1,1024,256]{2,1,0:T(8,128)}) async-done(((f32[1024,768]{1,0:T(8,128)}, f32[1,1024,256]{2,1,0:T(8,128)}), (f32[1024,768]{1,0:T(8,128)}, f32[1,1024,256]{2,1,0:T(8,128)})) %all-reduce.37.cloned.1.call-update) | async-done | bytes 4194320 | tf_op jit(solution)/shard_map/psum | solution.py:200
  752.1 6.2 fusion.121
  759.0 5.3 fusion.163
  764.4 188.5 %fusion.2 = f32[768,16]{0,1:T(8,128)S(1)} fusion(f32[768,768]{0,1:T(8,128)} %fusion.163), kind=kCustom, calls=%all-reduce-scatter | all-reduce-scatter fusion | flops 786433 | bytes 2408960
  960.7 10.8 collective-permute-start.9
  973.7 3.9 collective-permute-start.7
  981.8 4.0 collective-permute-start.4
  1000.4 5.8 concatenate.9
  1014.6 324.0 %all-reduce.27 = (f32[768]{0:T(1024)}, f32[4,768]{1,0:T(4,128)}, f32[4,256]{1,0:T(4,128)}, f32[768]{0:T(1024)}, f32[256]{0:T(256)}, /*index=5*/f32[12]{0:T(128)}, f32[12]{0:T(128)}, f32[12]{0:T(128)}, f32[768]{0:T(1024)}) all-reduce(f32[768]{0:T(1024)S(1)} %get-tuple-element.767, ...), channel_id=1, replica_groups=mesh['dp'=64,'tensor'=2] {'dp'}, use_global_device_ids=true, to_apply=%region_26.27 | all-reduce | flops 6692 | bytes 53536 | tf_op jit(solution)/shard_map/psum | solution.py:215
  1338.6 4.6 fusion.168
  1343.1 68.6 %all-reduce.35.cloned.1.call-done = f32[768,1804]{1,0:T(8,128)} async-done(((f32[768,1804]{1,0:T(8,128)}), f32[768,1804]{1,0:T(8,128)}) %all-reduce.35.cloned.1.call-update) | async-done | bytes 5541904
  (759 shorter events, 279.7 us)
Async XLA Ops:
  7.2 202.7 %copy-start = (bf16[768,768]{1,0:T(8,128)(2,1)S(1)}, bf16[768,768]{1,0:T(8,128)(2,1)}, u32[]{:S(2)}) copy-start(bf16[768,768]{1,0:T(8,128)(2,1)} %param.34) | copy-start | bytes 3538948
  7.2 302.8 %all-reduce.33.cloned.1.call-start = ((), (), s32[]{:S(2)}) async-start(), calls=%async_computation | async-start | bytes 6291456 | tf_op jit(solution)/shard_map/psum | solution.py:185
  9.5 304.8 %copy-start.82 = (f32[768]{0:T(1024)}, f32[768]{0:T(1024)S(1)}, u32[]{:S(2)}) copy-start(f32[768]{0:T(1024)S(1)} %convert_element_type.143) | copy-start | bytes 9220
  13.0 301.3 %copy-start.66 = (f32[768]{0:T(1024)}, f32[768]{0:T(1024)S(1)}, u32[]{:S(2)}) copy-start(f32[768]{0:T(1024)S(1)} %mul.1098) | copy-start | bytes 9220
  209.9 104.4 %copy-start.84 = (f32[1024]{0:T(1024)}, f32[1024]{0:T(1024)S(1)}, u32[]{:S(2)}) copy-start(f32[1024]{0:T(1024)S(1)} %add_rsqrt_fusion) | copy-start | bytes 12292
  214.9 531.5 %all-reduce.37.cloned.1.call-start = ((), (), s32[]{:S(2)}) async-start(), calls=%async_computation.2 | async-start | bytes 8388608 | tf_op jit(solution)/shard_map/psum | solution.py:200
  219.3 90.7 %copy-start.5 = (bf16[1,1024,768]{2,1,0:T(8,128)(2,1)S(1)}, bf16[1,1024,768]{2,1,0:T(8,128)(2,1)}, u32[]{:S(2)}) copy-start(bf16[1,1024,768]{2,1,0:T(8,128)(2,1)} %param.20) | copy-start | bytes 4718596
  384.1 26.6 %copy-start.15 = (f32[1,12,64,128]{3,2,1,0:T(8,128)S(1)}, f32[1,12,64,128]{3,2,1,0:T(8,128)}, u32[]{:S(2)}) copy-start(f32[1,12,64,128]{3,2,1,0:T(8,128)} %fusion.287) | copy-start | bytes 1179652 | tf_op jit(solution)/shard_map/transpose(jvp(vmap()))/while
  384.1 26.6 %copy-start.31 = (f32[4,1,256,12]{2,0,3,1:T(4,128)S(1)}, f32[4,1,256,12]{2,0,3,1:T(4,128)}, u32[]{:S(2)}) copy-start(f32[4,1,256,12]{2,0,3,1:T(4,128)} %copy-done.30) | copy-start | bytes 147460 | tf_op jit(solution)/shard_map/transpose(jvp(vmap()))/while
  446.4 26.6 %copy-start.15 = (f32[1,12,64,128]{3,2,1,0:T(8,128)S(1)}, f32[1,12,64,128]{3,2,1,0:T(8,128)}, u32[]{:S(2)}) copy-start(f32[1,12,64,128]{3,2,1,0:T(8,128)} %fusion.287) | copy-start | bytes 1179652 | tf_op jit(solution)/shard_map/transpose(jvp(vmap()))/while
  446.4 26.6 %copy-start.31 = (f32[4,1,256,12]{2,0,3,1:T(4,128)S(1)}, f32[4,1,256,12]{2,0,3,1:T(4,128)}, u32[]{:S(2)}) copy-start(f32[4,1,256,12]{2,0,3,1:T(4,128)} %copy-done.30) | copy-start | bytes 147460 | tf_op jit(solution)/shard_map/transpose(jvp(vmap()))/while
  446.4 26.6 %copy-start.33 = (f32[4,1,256,12]{2,0,3,1:T(4,128)S(1)}, f32[4,1,256,12]{2,0,3,1:T(4,128)}, u32[]{:S(2)}) copy-start(f32[4,1,256,12]{2,0,3,1:T(4,128)} %copy-done.32) | copy-start | bytes 147460 | tf_op jit(solution)/shard_map/transpose(jvp(vmap()))/while
  508.7 26.6 %copy-start.15 = (f32[1,12,64,128]{3,2,1,0:T(8,128)S(1)}, f32[1,12,64,128]{3,2,1,0:T(8,128)}, u32[]{:S(2)}) copy-start(f32[1,12,64,128]{3,2,1,0:T(8,128)} %fusion.287) | copy-start | bytes 1179652 | tf_op jit(solution)/shard_map/transpose(jvp(vmap()))/while
  508.7 26.6 %copy-start.31 = (f32[4,1,256,12]{2,0,3,1:T(4,128)S(1)}, f32[4,1,256,12]{2,0,3,1:T(4,128)}, u32[]{:S(2)}) copy-start(f32[4,1,256,12]{2,0,3,1:T(4,128)} %copy-done.30) | copy-start | bytes 147460 | tf_op jit(solution)/shard_map/transpose(jvp(vmap()))/while
  508.7 26.6 %copy-start.33 = (f32[4,1,256,12]{2,0,3,1:T(4,128)S(1)}, f32[4,1,256,12]{2,0,3,1:T(4,128)}, u32[]{:S(2)}) copy-start(f32[4,1,256,12]{2,0,3,1:T(4,128)} %copy-done.32) | copy-start | bytes 147460 | tf_op jit(solution)/shard_map/transpose(jvp(vmap()))/while
  508.7 26.6 %copy-start.97 = (s32[4,1]{0,1:T(1,128)S(1)}, s32[4,1]{0,1:T(1,128)}, u32[]{:S(2)}) copy-start(s32[4,1]{0,1:T(1,128)} %copy-done.96) | copy-start | bytes 52 | tf_op jit(solution)/shard_map/transpose(jvp(vmap()))/while
  571.0 26.6 %copy-start.15 = (f32[1,12,64,128]{3,2,1,0:T(8,128)S(1)}, f32[1,12,64,128]{3,2,1,0:T(8,128)}, u32[]{:S(2)}) copy-start(f32[1,12,64,128]{3,2,1,0:T(8,128)} %fusion.287) | copy-start | bytes 1179652 | tf_op jit(solution)/shard_map/transpose(jvp(vmap()))/while
  571.0 26.6 %copy-start.31 = (f32[4,1,256,12]{2,0,3,1:T(4,128)S(1)}, f32[4,1,256,12]{2,0,3,1:T(4,128)}, u32[]{:S(2)}) copy-start(f32[4,1,256,12]{2,0,3,1:T(4,128)} %copy-done.30) | copy-start | bytes 147460 | tf_op jit(solution)/shard_map/transpose(jvp(vmap()))/while
  630.2 116.1 %copy-start.8 = (f32[1024,256]{1,0:T(8,128)S(1)}, f32[1024,256]{1,0:T(8,128)}, u32[]{:S(2)}) copy-start(f32[1024,256]{1,0:T(8,128)} %copy-done.7) | copy-start | bytes 3145732
  630.2 116.1 %copy-start.19 = (f32[1,1024,256]{2,1,0:T(8,128)S(1)}, f32[1,1024,256]{2,1,0:T(8,128)}, u32[]{:S(2)}) copy-start(f32[1,1024,256]{2,1,0:T(8,128)} %get-tuple-element.862) | copy-start | bytes 3145732
  630.2 119.0 %copy-start.73 = (f32[1,256]{1,0:T(1,128)S(1)}, f32[1,256]{1,0:T(1,128)}, u32[]{:S(2)}) copy-start(f32[1,256]{1,0:T(1,128)} %copy-done.72) | copy-start | bytes 3076
  630.2 119.0 %copy-start.75 = (f32[1,256]{1,0:T(1,128)S(1)}, f32[1,256]{1,0:T(1,128)}, u32[]{:S(2)}) copy-start(f32[1,256]{1,0:T(1,128)} %copy-done.74) | copy-start | bytes 3076
  630.2 119.0 %copy-start.77 = (f32[1,256]{1,0:T(1,128)S(1)}, f32[1,256]{1,0:T(1,128)}, u32[]{:S(2)}) copy-start(f32[1,256]{1,0:T(1,128)} %copy-done.76) | copy-start | bytes 3076
  630.3 119.0 %copy-start.79 = (f32[1,256]{1,0:T(1,128)S(1)}, f32[1,256]{1,0:T(1,128)}, u32[]{:S(2)}) copy-start(f32[1,256]{1,0:T(1,128)} %copy-done.78) | copy-start | bytes 3076
  630.3 781.5 %all-reduce.35.cloned.1.call-start = ((), (), s32[]{:S(2)}) async-start(), calls=%async_computation.1 | async-start | bytes 11796480
  759.0 238.3 %copy-start.92 = (u32[128]{0:T(128)S(1)}, u32[128]{0:T(128)}, u32[]{:S(2)}) copy-start(u32[128]{0:T(128)} %constant.196) | copy-start | bytes 1540
  764.3 242.5 %copy-start.81 = (f32[768]{0:T(1024)S(1)}, f32[768]{0:T(1024)}, u32[]{:S(2)}) copy-start(f32[768]{0:T(1024)} %get-tuple-element.853) | copy-start | bytes 9220
  764.3 242.6 %copy-start.71 = (f32[768]{0:T(1024)S(1)}, f32[768]{0:T(1024)}, u32[]{:S(2)}) copy-start(f32[768]{0:T(1024)} %get-tuple-element.764) | copy-start | bytes 9220
  764.3 242.6 %copy-start.70 = (f32[768]{0:T(1024)S(1)}, f32[768]{0:T(1024)}, u32[]{:S(2)}) copy-start(f32[768]{0:T(1024)} %get-tuple-element.765) | copy-start | bytes 9220
  764.3 242.6 %copy-start.69 = (f32[768]{0:T(1024)S(1)}, f32[768]{0:T(1024)}, u32[]{:S(2)}) copy-start(f32[768]{0:T(1024)} %get-tuple-element.766) | copy-start | bytes 9220
  952.8 6.5 collective-permute-start.15
  954.1 6.5 collective-permute-start.14
  955.4 16.0 %collective-permute-start.13 = (f32[768,16]{0,1:T(8,128)S(1)}, f32[768,16]{0,1:T(8,128)S(1)}, u32[]{:S(2)}, u32[]{:S(2)}) collective-permute-start(f32[768,16]{0,1:T(8,128)S(1)} %fusion.2), channel_id=1, source_target_pairs={{0,28},{2,30},{4,32},{6,34},{8,36},{10,38},{12,40},{14,42},{16,44}... | collective-permute-start | bytes 147464
  956.7 16.9 %collective-permute-start.12 = (f32[768,16]{0,1:T(8,128)S(1)}, f32[768,16]{0,1:T(8,128)S(1)}, u32[]{:S(2)}, u32[]{:S(2)}) collective-permute-start(f32[768,16]{0,1:T(8,128)S(1)} %fusion.2), channel_id=1, source_target_pairs={{0,26},{2,28},{4,30},{6,32},{8,34},{10,36},{12,38},{14,40},{16,42}... | collective-permute-start | bytes 147464
  958.0 19.6 %collective-permute-start.11 = (f32[768,16]{0,1:T(8,128)S(1)}, f32[768,16]{0,1:T(8,128)S(1)}, u32[]{:S(2)}, u32[]{:S(2)}) collective-permute-start(f32[768,16]{0,1:T(8,128)S(1)} %fusion.2), channel_id=1, source_target_pairs={{0,24},{2,26},{4,28},{6,30},{8,32},{10,34},{12,36},{14,38},{16,40}... | collective-permute-start | bytes 147464
  959.3 20.6 %collective-permute-start.10 = (f32[768,16]{0,1:T(8,128)S(1)}, f32[768,16]{0,1:T(8,128)S(1)}, u32[]{:S(2)}, u32[]{:S(2)}) collective-permute-start(f32[768,16]{0,1:T(8,128)S(1)} %fusion.2), channel_id=1, source_target_pairs={{0,22},{2,24},{4,26},{6,28},{8,30},{10,32},{12,34},{14,36},{16,38}... | collective-permute-start | bytes 147464
  960.7 21.2 %collective-permute-start.9 = (f32[768,16]{0,1:T(8,128)S(1)}, f32[768,16]{0,1:T(8,128)S(1)}, u32[]{:S(2)}, u32[]{:S(2)}) collective-permute-start(f32[768,16]{0,1:T(8,128)S(1)} %fusion.2), channel_id=1, source_target_pairs={{0,20},{2,22},{4,24},{6,26},{8,28},{10,30},{12,32},{14,34},{16,36}... | collective-permute-start | bytes 147464
  971.5 14.3 %collective-permute-start.8 = (f32[768,16]{0,1:T(8,128)S(1)}, f32[768,16]{0,1:T(8,128)S(1)}, u32[]{:S(2)}, u32[]{:S(2)}) collective-permute-start(f32[768,16]{0,1:T(8,128)S(1)} %fusion.2), channel_id=1, source_target_pairs={{0,18},{2,20},{4,22},{6,24},{8,26},{10,28},{12,30},{14,32},{16,34}... | collective-permute-start | bytes 147464
  973.7 15.6 %collective-permute-start.7 = (f32[768,16]{0,1:T(8,128)S(1)}, f32[768,16]{0,1:T(8,128)S(1)}, u32[]{:S(2)}, u32[]{:S(2)}) collective-permute-start(f32[768,16]{0,1:T(8,128)S(1)} %fusion.2), channel_id=1, source_target_pairs={{0,16},{2,18},{4,20},{6,22},{8,24},{10,26},{12,28},{14,30},{16,32}... | collective-permute-start | bytes 147464
  977.6 14.2 collective-permute-start.6
  979.9 14.4 %collective-permute-start.5 = (f32[768,16]{0,1:T(8,128)S(1)}, f32[768,16]{0,1:T(8,128)S(1)}, u32[]{:S(2)}, u32[]{:S(2)}) collective-permute-start(f32[768,16]{0,1:T(8,128)S(1)} %fusion.2), channel_id=1, source_target_pairs={{0,12},{2,14},{4,16},{6,18},{8,20},{10,22},{12,24},{14,26},{16,28}... | collective-permute-start | bytes 147464
  981.8 17.3 %collective-permute-start.4 = (f32[768,16]{0,1:T(8,128)S(1)}, f32[768,16]{0,1:T(8,128)S(1)}, u32[]{:S(2)}, u32[]{:S(2)}) collective-permute-start(f32[768,16]{0,1:T(8,128)S(1)} %fusion.2), channel_id=1, source_target_pairs={{0,10},{2,12},{4,14},{6,16},{8,18},{10,20},{12,22},{14,24},{16,26}... | collective-permute-start | bytes 147464
  985.8 13.3 collective-permute-start.3
  989.3 9.9 collective-permute-start.2
  991.8 7.4 collective-permute-start.1
  994.3 6.1 collective-permute-start
  1011.7 326.9 %copy-start.65 = (f32[1024]{0:T(1024)S(1)}, f32[1024]{0:T(1024)}, u32[]{:S(2)}) copy-start(f32[1024]{0:T(1024)} %copy-done.64) | copy-start | bytes 12292
  1338.6 77.6 %copy-start.1 = (bf16[768,768]{1,0:T(8,128)(2,1)S(1)}, bf16[768,768]{1,0:T(8,128)(2,1)}, u32[]{:S(2)}) copy-start(bf16[768,768]{1,0:T(8,128)(2,1)} %param.34) | copy-start | bytes 3538948
  (129 other events, 933.4 us)
Sparse Core Ops, SparseCore 0:
  215.0 94.9 all-reduce.32
  630.3 115.9 all-reduce.36
  758.5 653.2 all-reduce.34
where the time goes:
time: 1440 us; the launch traced here: 1420 us
  blocking collectives  517 us (36%)
  local copies, waits for them, and re-layouts  312 us (22%)
  waiting for transfers between devices  272 us (19%)
  matrix products  152 us (11%)
  other arithmetic  86.1 us (6%)
  starting transfers between devices  44.3 us (3%)
  loops' own time  23.3 us (2%)
  between operations  16.5 us (1%)
    psum x1, blocking collectives, local(): lax.psum((normgain_local, grad_params[0], grad_params[1], convstate_local...  324 us
    unnamed x1, blocking collectives  188 us
    dynamic_update_slice x32, local copies, waits for them, and re-layouts, state_scan(): finished, outputs = lax.scan(jax.checkpoint(ssd_block), start, pieces)  163 us
    psum x1, waiting for transfers between devices, local(): lax.psum((input_part, grad_mix.reshape(row_count, state_cols)), 'tensor')  116 us
    psum x1, waiting for transfers between devices, local(): out_branch = lax.psum(rscale * local_part, 'tensor')  87.1 us
    unnamed x20, waiting for transfers between devices  68.7 us
    dot_general x12, matrix products, ssd_block(): jnp.einsum('tsh,shp->thp', weights, values, precision=lax.Precision.HIGHEST)  60.3 us
    unnamed x17, starting transfers between devices  44.2 us
  transfers between devices with their start and end apart: 19, of which 3 were waited for; matrix products, arithmetic and copies ran while one was open for 16% of the time, Pallas kernels for 0%

commit v1 on v0

v1 whole, which is shorter than its diff:
```python
import math

import jax
import jax.numpy as jnp
import numpy as np
from jax import lax
from jax.experimental import pallas as pl
from jax.experimental.pallas import tpu as pltpu
from jax.sharding import PartitionSpec as P

INNER = 1536
TAPS = 4
LANES = 128
HEAD = 64
STATE = 128
CHUNK = 256
HALO = 8
VMEM_BYTES = 56 * 1024 * 1024

epsilon = 1e-05
f32 = jnp.float32
bf16 = jnp.bfloat16

NN = ((1,), (0,))
NT = ((1,), (1,))
TN = ((0,), (0,))


def mm(left, right, dims=NN):
    return lax.dot_general(left, right, (dims, ((), ())), preferred_element_type=f32)


def lane_iota(shape):
    return lax.broadcasted_iota(jnp.int32, shape, 1)


def pack(values, heads):
    values = jnp.where(lane_iota(values.shape) < heads, values, 0.0)
    high = values.astype(bf16).astype(f32)
    rest = values - high
    middle = rest.astype(bf16).astype(f32)
    low = (rest - middle).astype(bf16).astype(f32)
    return (high + pltpu.roll(middle, 16, 1) + pltpu.roll(low, 32, 1)).astype(bf16)


def unpack(values):
    return values + pltpu.roll(values, LANES - 16, 1) + pltpu.roll(values, LANES - 32, 1)


def spread_heads(values, expand, heads):
    return mm(pack(values, heads), expand)


def sum_heads(values, collect):
    high = values.astype(bf16)
    low = (values - high.astype(f32)).astype(bf16)
    return mm(high, collect) + mm(low, collect)


def sigmoid(values):
    return 1.0 / (1.0 + jnp.exp(-values))


def softplus(values):
    return jnp.maximum(values, 0.0) + jnp.log1p(jnp.exp(-jnp.abs(values)))


def half_tile(values, half):
    lane = lane_iota(values.shape)
    keep = lane < HEAD if half == 0 else lane >= HEAD
    return jnp.where(keep, values, jnp.zeros_like(values))


def norm_scale(data):
    return lax.rsqrt(jnp.mean(data * data, axis=1, keepdims=True) + epsilon)


def scan_sizes(raw_step, step_bias, neg_rate, aux, heads, length):
    step = softplus(raw_step + step_bias)
    logdecay = step * neg_rate
    places = lax.broadcasted_iota(jnp.int32, (length, length), 0)
    others = lax.broadcasted_iota(jnp.int32, (length, length), 1)
    lower = (places >= others).astype(bf16)
    cumlog = unpack(mm(lower, pack(logdecay, heads)))
    entry = aux[:, 7:8] * jnp.exp(cumlog)
    back = aux[:, 8:9] * jnp.exp(cumlog[length - 1 : length] - cumlog)
    return step, logdecay, cumlog, entry, back


def forward_kernel(heads, tokens, aux, seg_row, cotangent, norm_gain, wall, taps, tap_bias,
                   step_bias, neg_rate, skip, gate_gain, out_proj, expand,
                   normed_out, raw_out, pre_out, y_out, scaled_out, partial_out, stats_out,
                   state_out, state, halo):
    length = tokens.shape[0]
    width = gate_gain.shape[1]
    mixed_width = width + 2 * STATE

    @pl.when(pl.program_id(0) == 0)
    def _():
        state[...] = jnp.zeros_like(state)
        halo[0:HALO, :] = jnp.zeros((HALO, mixed_width), f32)

    data = tokens[...].astype(f32)
    normed = (data * norm_scale(data) * norm_gain[...]).astype(bf16)
    normed_out[...] = normed
    raw = mm(normed, wall[...])
    raw_out[...] = raw
    mixer = raw[:, width : width + mixed_width]
    halo[HALO : HALO + length, :] = mixer
    masks = aux[...]
    pre = tap_bias[...] + mixer * taps[TAPS - 1 : TAPS, :]
    for offset in range(1, TAPS):
        moved = halo[HALO - offset : HALO - offset + length, :]
        pre += moved * taps[TAPS - 1 - offset : TAPS - offset, :] * masks[:, offset : offset + 1]
    halo[0:HALO, :] = halo[length : length + HALO, :]
    pre_out[...] = pre
    act = pre * sigmoid(pre)
    values = act[:, :width]
    write = act[:, width : width + STATE].astype(bf16)
    read = act[:, width + STATE :].astype(bf16)
    step, _, cumlog, entry, back = scan_sizes(
        raw[:, width + mixed_width :], step_bias[...], neg_rate[...], masks, heads, length
    )
    entry_wide = spread_heads(entry, expand[...], heads)
    back_wide = spread_heads(back, expand[...], heads)
    stepped = values * spread_heads(step, expand[...], heads)
    before = state[...]
    state_out[0] = before
    across = mm(read, before.astype(bf16)) * entry_wide
    state[...] = before * entry_wide[length - 1 : length, :] + mm(
        write, (stepped * back_wide).astype(bf16), TN
    )
    similar = mm(read, write, NT)
    places = lax.broadcasted_iota(jnp.int32, (length, length), 0)
    others = lax.broadcasted_iota(jnp.int32, (length, length), 1)
    open_pair = (masks[:, 0:1] == seg_row[...]) & (places >= others)
    shut = jnp.where(open_pair, 0.0, -1e30)
    cum_rows = jnp.transpose(cumlog)
    stepped_low = stepped.astype(bf16)
    tiles = []
    for pair in range(heads // 2):
        tile = stepped_low[:, pair * LANES : (pair + 1) * LANES]
        total = None
        for half in range(2):
            head = 2 * pair + half
            decay = jnp.exp(cumlog[:, head : head + 1] - cum_rows[head : head + 1, :] + shut)
            term = mm((decay * similar).astype(bf16), half_tile(tile, half))
            total = term if total is None else total + term
        tiles.append(total)
    y = jnp.concatenate(tiles, axis=1) + across + skip[...] * values
    y_out[...] = y
    gate = raw[:, :width]
    gated = y * (gate * sigmoid(gate))
    squares = jnp.sum(gated * gated, axis=1, keepdims=True)
    scaled = (gated * gate_gain[...]).astype(bf16)
    scaled_out[...] = scaled
    partial = mm(scaled, out_proj[...])
    partial_out[...] = partial
    along = jnp.sum(cotangent[...].astype(f32) * partial, axis=1, keepdims=True)
    lane = lane_iota((length, LANES))
    stats = jnp.where(lane == 0, squares, jnp.where(lane == 1, along, 0.0))
    stats_out[...] = jnp.transpose(stats)[0:8, :]


def backward_kernel(heads, tokens, aux, seg_row, cotangent, norm_gain, wall, taps,
                    step_bias, neg_rate, skip, gate_gain, out_proj, expand, collect,
                    raw_in, pre_in, y_in, scales, state_in,
                    back_out, joined_out, grad_norm, grad_taps,
                    grad_heads, grad_gate, state_grad, halo):
    length = tokens.shape[0]
    width = gate_gain.shape[1]
    mixed_width = width + 2 * STATE

    @pl.when(pl.program_id(0) == 0)
    def _():
        state_grad[...] = jnp.zeros_like(state_grad)
        halo[length : length + HALO, :] = jnp.zeros((HALO, mixed_width), f32)
        for member in (grad_norm, grad_taps, grad_heads, grad_gate):
            member[...] = jnp.zeros_like(member)

    masks = aux[...]
    columns = jnp.transpose(jnp.concatenate([scales[...], jnp.zeros((LANES - 8, length), f32)], 0))
    rscale = columns[:, 0:1]
    ratio = columns[:, 1:2]
    grad_part = (rscale * cotangent[...].astype(f32)).astype(bf16)
    grad_scaled = mm(grad_part, out_proj[...], NT)
    gate = raw_in[:, :width]
    gate_sig = sigmoid(gate)
    gate_silu = gate * gate_sig
    y = y_in[...]
    gated = y * gate_silu
    grad_gate[0:1, :] += jnp.sum(grad_scaled * gated, axis=0, keepdims=True)
    grad_gated = grad_scaled * gate_gain[...] - ratio * gated * (1.0 / INNER)
    grad_y = grad_gated * gate_silu
    grad_z = grad_gated * y * (gate_sig * (1.0 + gate * (1.0 - gate_sig)))

    pre = pre_in[...]
    pre_sig = sigmoid(pre)
    act = pre * pre_sig
    values = act[:, :width]
    write = act[:, width : width + STATE].astype(bf16)
    read = act[:, width + STATE :].astype(bf16)
    raw_step = raw_in[:, width + mixed_width :]
    step, logdecay, cumlog, entry, back = scan_sizes(
        raw_step, step_bias[...], neg_rate[...], masks, heads, length
    )
    entry_wide = spread_heads(entry, expand[...], heads)
    back_wide = spread_heads(back, expand[...], heads)
    step_wide = spread_heads(step, expand[...], heads)
    stepped = values * step_wide
    before = state_in[0]
    before_low = before.astype(bf16)
    after_grad = state_grad[...]
    after_low = after_grad.astype(bf16)
    grad_entry = grad_y * entry_wide
    grad_entry_low = grad_entry.astype(bf16)
    grad_y_low = grad_y.astype(bf16)
    stepped_low = stepped.astype(bf16)
    stepped_back = stepped * back_wide
    from_entry = sum_heads(grad_entry * mm(read, before_low), collect[...])
    grad_read = mm(grad_entry_low, before_low, NT)
    carried = mm(write, after_low)
    from_back = sum_heads(stepped_back * carried, collect[...])
    grad_write = mm(stepped_back.astype(bf16), after_low, NT)
    overlap = jnp.sum(before * after_grad, axis=0, keepdims=True) * entry_wide[length - 1 : length, :]
    overlap = sum_heads(jnp.broadcast_to(overlap, (8, width)), collect[...])[0:1, :]
    state_grad[...] = after_grad * entry_wide[length - 1 : length, :] + mm(read, grad_entry_low, TN)

    similar = mm(write, read, NT)
    places = lax.broadcasted_iota(jnp.int32, (length, length), 0)
    others = lax.broadcasted_iota(jnp.int32, (length, length), 1)
    open_pair = (masks[:, 0:1] == seg_row[...]) & (places <= others)
    shut = jnp.where(open_pair, 0.0, -1e30)
    cum_rows = jnp.transpose(cumlog)
    lane = lane_iota((length, LANES))
    grad_similar = jnp.zeros((length, length), f32)
    from_source = jnp.zeros((length, LANES), f32)
    target_rows = []
    tiles = []
    for pair in range(heads // 2):
        span = slice(pair * LANES, (pair + 1) * LANES)
        total = None
        for half in range(2):
            head = 2 * pair + half
            decay = jnp.exp(cum_rows[head : head + 1, :] - cumlog[:, head : head + 1] + shut)
            weights = decay * similar
            grad_half = half_tile(grad_y_low[:, span], half)
            term = mm(weights.astype(bf16), grad_half)
            total = term if total is None else total + term
            grad_decayed = mm(stepped_low[:, span], grad_half, NT)
            grad_similar += grad_decayed * decay
            product = grad_decayed * weights
            from_source = jnp.where(lane == head, jnp.sum(product, axis=1, keepdims=True), from_source)
            target_rows.append(jnp.sum(product, axis=0, keepdims=True))
        tiles.append(total)
    target_rows.append(jnp.zeros((LANES - heads, length), f32))
    from_target = jnp.transpose(jnp.concatenate(target_rows, axis=0))
    grad_similar_low = grad_similar.astype(bf16)
    grad_write += mm(grad_similar_low, read)
    grad_read += mm(grad_similar_low, write, TN)
    grad_stepped = jnp.concatenate(tiles, axis=1) + back_wide * carried

    grad_cumlog = from_entry - from_back + from_target - from_source
    upper = (places <= others).astype(bf16)
    grad_log = unpack(mm(upper, pack(grad_cumlog, heads)))
    grad_log += jnp.sum(from_back, axis=0, keepdims=True) + overlap
    grad_log = jnp.where(lane < heads, grad_log, 0.0)
    grad_step = sum_heads(grad_stepped * values, collect[...]) + neg_rate[...] * grad_log
    grad_rawstep = grad_step * sigmoid(raw_step + step_bias[...])
    grad_heads[0:1, :] += jnp.sum(grad_rawstep, axis=0, keepdims=True)
    grad_heads[1:2, :] += jnp.sum(grad_log * logdecay, axis=0, keepdims=True)
    skipped = jnp.sum(grad_y * values, axis=0, keepdims=True)
    grad_heads[2:3, :] += sum_heads(jnp.broadcast_to(skipped, (8, width)), collect[...])[0:1, :]
    grad_values = grad_stepped * step_wide + skip[...] * grad_y
    grad_pre = jnp.concatenate([grad_values, grad_write, grad_read], axis=1) * (
        pre_sig * (1.0 + pre * (1.0 - pre_sig))
    )
    halo[0:length, :] = grad_pre
    mixer = raw_in[:, width : width + mixed_width]
    grad_mixer = grad_pre * taps[TAPS - 1 : TAPS, :]
    grad_taps[TAPS - 1 : TAPS, :] += jnp.sum(grad_pre * mixer, axis=0, keepdims=True)
    grad_taps[TAPS : TAPS + 1, :] += jnp.sum(grad_pre, axis=0, keepdims=True)
    for offset in range(1, TAPS):
        place = TAPS - 1 - offset
        moved = halo[offset : offset + length, :] * masks[:, 3 + offset : 4 + offset]
        grad_mixer += moved * taps[place : place + 1, :]
        grad_taps[place : place + 1, :] += jnp.sum(moved * mixer, axis=0, keepdims=True)
    halo[length : length + HALO, :] = halo[0:HALO, :]
    joined = jnp.concatenate(
        [grad_z.astype(bf16), grad_mixer.astype(bf16), grad_rawstep.astype(bf16)], axis=1
    )
    grad_input = mm(joined, wall[...], NT)
    joined_out[...] = joined
    data = tokens[...].astype(f32)
    scale = norm_scale(data)
    grad_norm[0:1, :] += jnp.sum(grad_input * data * scale, axis=0, keepdims=True)
    gained = grad_input * norm_gain[...]
    back_out[...] = gained * scale - data * (
        scale * scale * scale * jnp.mean(gained * data, axis=1, keepdims=True)
    )


def side_columns(segment, chunk):
    length = segment.shape[0]
    columns = [segment]
    before = jnp.concatenate([jnp.full((TAPS - 1,), -1, jnp.int32), segment])
    after = jnp.concatenate([segment, jnp.full((TAPS - 1,), -1, jnp.int32)])
    for offset in range(1, TAPS):
        columns.append(before[TAPS - 1 - offset : TAPS - 1 - offset + length] == segment)
    for offset in range(1, TAPS):
        columns.append(after[offset : offset + length] == segment)
    blocks = segment.reshape(length // chunk, chunk)
    last = blocks[:, chunk - 1]
    prior = jnp.concatenate([jnp.full((1,), -1, jnp.int32), last[:-1]])
    columns.append((blocks == prior[:, None]).reshape(length))
    columns.append((blocks == last[:, None]).reshape(length))
    stacked = jnp.stack([member.astype(f32) for member in columns], axis=1)
    return jnp.pad(stacked, ((0, 0), (0, LANES - len(columns))))


def pad_heads(values):
    return jnp.pad(values, (0, LANES - values.shape[0])).reshape(1, LANES)


def local(
    tokens,
    segment_ids,
    norm_gain,
    proj_main,
    proj_state,
    proj_step,
    conv_main,
    conv_state,
    bias_main,
    bias_state,
    step_bias,
    log_rate,
    skip_gain,
    gate_gain,
    out_proj,
    cotangent,
):
    packs, length, model = tokens.shape
    width = proj_main.shape[2]
    heads = step_bias.shape[0]
    state_cols = proj_state.shape[1]
    mixed_width = width + state_cols
    wall_cols = width + mixed_width + LANES
    chunk = min(CHUNK, length)
    count = length // chunk
    data = tokens.reshape(length, model)
    cot = cotangent.reshape(length, model)
    wall = jnp.concatenate(
        [
            proj_main[:, 0],
            proj_main[:, 1],
            proj_state,
            jnp.pad(proj_step, ((0, 0), (0, LANES - heads))),
        ],
        axis=1,
    )
    taps = jnp.concatenate([conv_main, conv_state], axis=1)
    tap_bias = jnp.concatenate([bias_main, bias_state]).reshape(1, mixed_width)
    step_row = pad_heads(step_bias)
    neg_rate = pad_heads(-jnp.exp(log_rate))
    skip = jnp.repeat(skip_gain, HEAD).reshape(1, width)
    gain_row = norm_gain.astype(f32).reshape(1, model)
    gate_row = gate_gain.astype(f32).reshape(1, width)
    aux = side_columns(segment_ids[0], chunk)
    seg_row = segment_ids.astype(f32)
    places = np.arange(LANES)[:, None]
    owner = np.arange(width)[None, :] // HEAD
    expand = jnp.asarray((places % 16 == owner) & (places < 48), bf16)
    collect = jnp.asarray((places == owner).T, bf16)

    def whole(shape):
        return pl.BlockSpec(shape, lambda i: (0,) * len(shape))

    def specs(order):
        def rows(cols):
            return pl.BlockSpec((chunk, cols), lambda i: (order(i), 0))

        def wide(count_rows):
            return pl.BlockSpec((count_rows, chunk), lambda i: (0, order(i)))

        state = pl.BlockSpec((1, STATE, width), lambda i: (order(i), 0, 0))
        return rows, wide, state

    params = pltpu.CompilerParams(
        dimension_semantics=("arbitrary",), vmem_limit_bytes=VMEM_BYTES
    )
    rows, wide, state_spec = specs(lambda i: i)
    normed, raw, pre, y, scaled, partial, stats, states = pl.pallas_call(
        lambda *refs: forward_kernel(heads, *refs),
        grid=(count,),
        in_specs=[
            rows(model), rows(LANES), wide(1), rows(model), whole((1, model)),
            whole((model, wall_cols)), whole((TAPS, mixed_width)), whole((1, mixed_width)),
            whole((1, LANES)), whole((1, LANES)), whole((1, width)), whole((1, width)),
            whole((width, model)), whole((LANES, width)),
        ],
        out_specs=[
            rows(model), rows(wall_cols), rows(mixed_width), rows(width), rows(width),
            rows(model), wide(8), state_spec,
        ],
        out_shape=[
            jax.ShapeDtypeStruct((length, model), bf16),
            jax.ShapeDtypeStruct((length, wall_cols), f32),
            jax.ShapeDtypeStruct((length, mixed_width), f32),
            jax.ShapeDtypeStruct((length, width), f32),
            jax.ShapeDtypeStruct((length, width), bf16),
            jax.ShapeDtypeStruct((length, model), f32),
            jax.ShapeDtypeStruct((8, length), f32),
            jax.ShapeDtypeStruct((count, STATE, width), f32),
        ],
        scratch_shapes=[
            pltpu.VMEM((STATE, width), f32),
            pltpu.VMEM((chunk + HALO, mixed_width), f32),
        ],
        compiler_params=params,
        cost_estimate=pl.CostEstimate(
            flops=15_000_000_000, bytes_accessed=30_000_000, transcendentals=5_000_000
        ),
    )(data, aux, seg_row, cot, gain_row, wall, taps, tap_bias, step_row, neg_rate, skip,
      gate_row, out_proj, expand)

    swap = [(0, 1), (1, 0)]
    totals = stats[:2] + lax.ppermute(stats[:2], "tensor", swap)
    rscale = lax.rsqrt(totals[0] / INNER + epsilon)
    ratio = totals[1] * rscale * rscale * rscale
    scales = jnp.pad(jnp.stack([rscale, ratio]), ((0, 6), (0, 0)))
    other = lax.ppermute(partial, "tensor", swap)

    cot_wide = cot.astype(f32)
    grad_part = (rscale[:, None] * cot_wide).astype(bf16)
    grad_outproj = scatter_sum(grad_part, scaled, "xyz")

    rows, wide, state_spec = specs(lambda i: count - 1 - i)
    back, joined, grad_norm, grad_taps, grad_heads, grad_gate = pl.pallas_call(
        lambda *refs: backward_kernel(heads, *refs),
        grid=(count,),
        in_specs=[
            rows(model), rows(LANES), wide(1), rows(model), whole((1, model)),
            whole((model, wall_cols)), whole((TAPS, mixed_width)),
            whole((1, LANES)), whole((1, LANES)), whole((1, width)), whole((1, width)),
            whole((width, model)), whole((LANES, width)), whole((width, LANES)),
            rows(wall_cols), rows(mixed_width), rows(width), wide(8), state_spec,
        ],
        out_specs=[
            rows(model), rows(wall_cols), whole((8, model)),
            whole((8, mixed_width)), whole((8, LANES)), whole((8, width)),
        ],
        out_shape=[
            jax.ShapeDtypeStruct((length, model), f32),
            jax.ShapeDtypeStruct((length, wall_cols), bf16),
            jax.ShapeDtypeStruct((8, model), f32),
            jax.ShapeDtypeStruct((8, mixed_width), f32),
            jax.ShapeDtypeStruct((8, LANES), f32),
            jax.ShapeDtypeStruct((8, width), f32),
        ],
        scratch_shapes=[
            pltpu.VMEM((STATE, width), f32),
            pltpu.VMEM((chunk + HALO, mixed_width), f32),
        ],
        compiler_params=params,
        cost_estimate=pl.CostEstimate(
            flops=30_000_000_000, bytes_accessed=60_000_000, transcendentals=6_000_000
        ),
    )(data, aux, seg_row, cot, gain_row, wall, taps, step_row, neg_rate, skip, gate_row,
      out_proj, expand, collect, raw, pre, y, scales, states)

    mixed = (data.astype(f32) + rscale[:, None] * (partial + other)).astype(bf16)
    back_sum = back + lax.ppermute(back, "tensor", swap)
    grad_tokens = (cot_wide + back_sum).astype(bf16)

    wall_pad = -wall_cols % (2 * LANES)
    reduced = scatter_sum(normed, jnp.pad(joined, ((0, 0), (0, wall_pad))), "yxz")
    grad_state = reduced[:, 2 * width : width + mixed_width]
    grad_state = grad_state + lax.ppermute(grad_state, "tensor", swap)

    own = [grad_taps[:, :width], grad_heads, grad_gate]
    shared = jnp.concatenate([grad_norm, grad_taps[:, width:]], axis=1)
    shared = shared + lax.ppermute(shared, "tensor", swap)
    summed = share_sum(jnp.concatenate([*own, shared], axis=1)[:5])
    cuts = np.cumsum([width, LANES, width, model])
    own_taps, own_heads, own_gate, norm_part, shared_taps = jnp.split(summed, cuts, axis=1)
    return (
        mixed.reshape(tokens.shape),
        grad_tokens.reshape(tokens.shape),
        norm_part[0],
        reduced[:, : 2 * width].reshape(-1, 2, width),
        grad_state,
        reduced[:, width + mixed_width : width + mixed_width + heads],
        own_taps[:TAPS],
        shared_taps[:TAPS],
        own_taps[TAPS],
        shared_taps[TAPS],
        own_heads[0, :heads],
        own_heads[1, :heads],
        own_heads[2, :heads],
        own_gate[0],
        grad_outproj.T,
    )


RINGS = (("y", 4), ("z", 2), ("x", 4), ("core", 2))


def ring_place(index, ring):
    for name, size in reversed(RINGS):
        if name == ring:
            return index % size
        index = index // size


def ring_shift(values, ring, step):
    pairs = []
    for source in range(math.prod(size for _, size in RINGS)):
        stride = 1
        for name, size in reversed(RINGS):
            if name == ring:
                place = source // stride % size
                pairs.append((source, source + ((place + step) % size - place) * stride))
            stride *= size
    return lax.ppermute(values, "dp", pairs)


def scatter_sum(left, right, order):
    index = lax.axis_index("dp")
    core = ring_place(index, "core")
    half = right.shape[1] // 2

    def product(which):
        return mm(left, lax.dynamic_slice_in_dim(right, which * half, half, axis=1), TN)

    away = ring_shift(product(1 - core), "core", 1)
    total = product(core) + away
    sizes = dict(RINGS)
    rings = [name for name, _ in RINGS if name != "core"]
    rows = total.shape[0] // math.prod(sizes[name] for name in rings)
    total = total.reshape([sizes[name] for name in rings] + [rows, half])
    for ring in order:
        axis, size = rings.index(ring), sizes[ring]
        place = ring_place(index, ring)
        parts = [
            lax.dynamic_index_in_dim(total, (place + step) % size, axis, keepdims=False)
            for step in range(size)
        ]
        total = parts[0]
        for step in range(1, size):
            total = total + ring_shift(parts[step], ring, step)
        rings.remove(ring)
    share = rows // 2
    mine = lax.dynamic_slice_in_dim(total, core * share, share, axis=0)
    other = lax.dynamic_slice_in_dim(total, (1 - core) * share, share, axis=0)
    other = ring_shift(other, "core", 1)
    return jnp.where(
        core == 0,
        jnp.concatenate([mine, other], axis=1),
        jnp.concatenate([other, mine], axis=1),
    )


def share_sum(values):
    for ring, size in reversed(RINGS):
        moved = [ring_shift(values, ring, step) for step in range(1, size)]
        for member in moved:
            values = values + member
    return values


def solution(mesh):
    placed = (
        P("dp", None, None),
        P("dp", None),
        P(),
        P(None, None, "tensor"),
        P(),
        P(None, "tensor"),
        P(None, "tensor"),
        P(),
        P("tensor"),
        P(),
        P("tensor"),
        P("tensor"),
        P("tensor"),
        P("tensor"),
        P("tensor", None),
        P("dp", None, None),
    )
    return jax.shard_map(
        local,
        mesh=mesh,
        in_specs=placed,
        out_specs=(
            P("dp", None, None),
            P("dp", None, None),
            P(),
            P("dp", None, "tensor"),
            P("dp", None),
            P("dp", "tensor"),
            P(None, "tensor"),
            P(),
            P("tensor"),
            P(),
            P("tensor"),
            P("tensor"),
            P("tensor"),
            P("tensor"),
            P("tensor", "dp"),
        ),
        check_vma=False,
    )
```

time: 1440 us -> 283 us (0.20); the launches traced: 1420 us -> 281 us
  blocking collectives: 517 us -> 0 us
  local copies, waits for them, and re-layouts: 312 us -> 24.2 us
  waiting for transfers between devices: 272 us -> 123 us
  matrix products: 152 us -> 14.9 us
  other arithmetic: 86.1 us -> 15.7 us
  Pallas kernels: 0 us -> 60.2 us
  loops' own time: 23.3 us -> 0 us
  between operations: 16.5 us -> 1.18 us
    psum x2 -> x0, blocking collectives: 329 us -> none  [the longest x1 324 us: local(): lax.psum((normgain_local, grad_params[0], grad_params[1], convstate_local...]
    psum x2 -> x0, waiting for transfers between devices: 203 us -> none  [the longest x1 116 us: local(): lax.psum((input_part, grad_mix.reshape(row_count, state_cols)), 'tensor')]
    unnamed x1 -> x0, blocking collectives: 188 us -> none
    dynamic_update_slice x32 -> x0, local copies, waits for them, and re-layouts: 163 us -> none  [state_scan(): finished, outputs = lax.scan(jax.checkpoint(ssd_block), start, pieces)]
    dot_general x66 -> x4, matrix products: 152 us -> 14.9 us  [mm(): lax.dot_general(left, right, (dims, ((), ())), preferred_element_type=f32)]
    ppermute x0 -> x31, waiting for transfers between devices: none -> 123 us  [the longest x26 121 us: ring_shift(): return lax.ppermute(values, 'dp', pairs)]
    unnamed x20 -> x0, waiting for transfers between devices: 68.7 us -> none
    pallas_call x0 -> x2, Pallas kernels: none -> 60.2 us  [the longest x1 37.2 us: local(): pl.pallas_call(lambda *refs: backward_kernel(heads, *refs), grid=(count,)...]
  transfers between devices with their start and end apart: 19 -> 31, of which waited for: 3 -> 10; matrix products, arithmetic and copies ran while one was open for 16% -> 10% of each run, Pallas kernels for 0% -> 0%
where the time goes in v1:
time: 283 us; the launch traced here: 281 us
  waiting for transfers between devices  123 us (43%)
  Pallas kernels  60.2 us (21%)
  starting transfers between devices  42.1 us (15%)
  local copies, waits for them, and re-layouts  24.2 us (9%)
  other arithmetic  15.7 us (6%)
  matrix products  14.9 us (5%)
    ppermute x26, waiting for transfers between devices, ring_shift(): return lax.ppermute(values, 'dp', pairs)  121 us
    pallas_call x1, Pallas kernels, local(): pl.pallas_call(lambda *refs: backward_kernel(heads, *refs), grid=(count,)...  37.2 us
    ppermute x26, starting transfers between devices, ring_shift(): return lax.ppermute(values, 'dp', pairs)  36.8 us
    pallas_call x1, Pallas kernels, local(): pl.pallas_call(lambda *refs: forward_kernel(heads, *refs), grid=(count,),...  23 us
    dot_general x4, matrix products, mm(): lax.dot_general(left, right, (dims, ((), ())), preferred_element_type=f32)  14.9 us
    slice x1, local copies, waits for them, and re-layouts, local(): proj_main[:, 0]  7.93 us
  transfers between devices with their start and end apart: 31, of which 10 were waited for; matrix products, arithmetic and copies ran while one was open for 10% of the time, Pallas kernels for 0%

profile of v1, /device:TPU:0, one launch (start us, length us, event | category | flops | bytes accessed | tf_op | source)
XLA Modules:
  0.0 281.3 jit_solution(11372457615702738506)
XLA Ops:
  1.2 2.0 fusion.49
  3.3 1.0 fusion.35
  5.8 1.3 reshape.161.refs_4_
  7.0 0.9 copy.59
  8.0 7.9 %fusion.48 = (bf16[768,1,768]{2,1,0:T(2,128)(2,1)S(1)}, bf16[768,1,768]{2,1,0:T(2,128)(2,1)}) fusion(bf16[768,2,768]{2,1,0:T(2,128)(2,1)} %param.21), kind=kLoop, calls=%fused_computation.116 | loop fusion | bytes 4718592 | tf_op jit(solution)/shard_map/slice | solution.py:355
  17.3 0.8 pad.25.refs_1_
  18.2 2.1 copy_bitcast_fusion
  21.4 1.7 fusion.3.refs_5_
  23.1 23.0 %shard_map.289 = (bf16[1024,768]{1,0:T(8,128)(2,1)}, f32[1024,1920]{1,0:T(8,128)}, f32[1024,1024]{1,0:T(8,128)}, f32[1024,768]{1,0:T(8,128)}, bf16[1024,768]{1,0...) custom-call(bf16[1024,768]{1,0:T(8,128)(2,1)} %bitcast.122, ...), custom_call_target="tpu_custom_call" | custom-call | flops 15000000512 | bytes 30000000 | tf_op jit(solution)/shard_map/pallas_call | solution.py:393
  46.9 2.0 collective-permute-start
  48.9 1.6 collective-permute-done
  52.0 37.2 %shard_map.290 = (f32[1024,768]{1,0:T(8,128)}, bf16[1024,1920]{1,0:T(8,128)(2,1)}, f32[8,768]{1,0:T(8,128)}, f32[8,1024]{1,0:T(8,128)}, f32[8,128]{1,0:T(8,128)}, /*index=5*/f32[8,768]{1,0:T(8,128)}) custom-call(bf16[1024,768]{1,0:T(8,128)(2,1)} %bitcast.123, f32[1024,128]{1,0:T(8,128)} %pad.25.refs_1_, f32[1,1024]{1,0:T(1,128)} %get-tuple-element.69.refs_2_, ...), custom_call_target="tpu_custom_call" | custom-call | flops 30000001024 | bytes 60000000 | tf_op jit(solution)/shard_map/pallas_call | solution.py:439
  90.6 2.0 collective-permute-start.3
  92.6 5.1 %fusion.5 = f32[768,1024]{1,0:T(8,128)} fusion(bf16[1024,768]{1,0:T(8,128)(2,1)S(1)} %copy-done.5, s32[]{:T(128)S(6)} %select_n.191, bf16[1024,1920]{1,0:T(8,128)(2,1)} %get-tuple-element.41), kind=kOutput, calls=%fused_computation.11 | convolution fusion | flops 1610612736 | bytes 8650756 | tf_op jit(solution)/shard_map/dot_general | solution.py:30
  97.8 2.2 fusion.11
  100.7 3.0 %collective-permute-done.4 = f32[5,2688]{1,0:T(8,128)S(1)} collective-permute-done((f32[5,2688]{1,0:T(8,128)S(1)}, f32[5,2688]{1,0:T(8,128)S(1)}, u32[]{:S(2)}, u32[]{:S(2)}) %collective-permute-start.4) | collective-permute-done | bytes 53792 | tf_op jit(solution)/shard_map/ppermute | solution.py:525
  103.7 2.8 %collective-permute-start.7 = (f32[5,2688]{1,0:T(8,128)S(1)}, f32[5,2688]{1,0:T(8,128)S(1)}, u32[]{:S(2)}, u32[]{:S(2)}) collective-permute-start(f32[5,2688]{1,0:T(8,128)S(1)} %fusion.46), channel_id=1, source_target_pairs={{0,12},{2,14},{4,0},{6,2},{8,4},{10,6},{12,8},{14,10},{16,28},{18,... | collective-permute-start | bytes 161288 | tf_op jit(solution)/shard_map/ppermute | solution.py:525
  106.5 0.8 collective-permute-start.6
  107.4 0.9 collective-permute-start.5
  108.2 3.1 %convolution_add_fusion = f32[768,384]{1,0:T(8,128)S(1)} fusion(f32[768,384]{1,0:T(8,128)} %collective-permute-done.22, bf16[1024,768]{1,0:T(8,128)(2,1)} %get-tuple-element.42, s32[]{:T(128)S(6)} %select_n.222, f32[1024]{0:T(1024)S(1)} %bitcast.127, bf16[1,1024,768]{2,1,0:T(8,128)(2,1)} %param.33), kind=kOutput, calls=%fused_computation.15 | convolution fusion | flops 606633984 | bytes 4722692 | tf_op jit(solution)/shard_map/dot_general | solution.py:30
  111.4 1.0 copy-done.7
  112.4 0.9 dynamic-slice_bitcast_fusion.5
  113.3 2.4 collective-permute-start.25
  115.6 1.5 collective-permute-start.24
  117.2 3.7 %collective-permute-start.8 = (f32[5,2688]{1,0:T(8,128)S(1)}, f32[5,2688]{1,0:T(8,128)}, u32[]{:S(2)}, u32[]{:S(2)}) collective-permute-start(f32[5,2688]{1,0:T(8,128)S(1)} %add_add_fusion.1), channel_id=1, source_target_pairs={{0,16},{2,18},{4,20},{6,22},{8,24},{10,26},{12,28},{14,30},{16,0},... | collective-permute-start | bytes 161288 | tf_op jit(solution)/shard_map/ppermute | solution.py:525
  120.8 2.9 %collective-permute-done.8 = f32[5,2688]{1,0:T(8,128)} collective-permute-done((f32[5,2688]{1,0:T(8,128)S(1)}, f32[5,2688]{1,0:T(8,128)}, u32[]{:S(2)}, u32[]{:S(2)}) %collective-permute-start.8) | collective-permute-done | bytes 53792 | tf_op jit(solution)/shard_map/ppermute | solution.py:525
  123.7 0.9 add.288
  124.6 3.5 %collective-permute-done.25 = f32[4,2,24,384]{3,2,1,0:T(8,128)} collective-permute-done((f32[4,2,24,384]{3,2,1,0:T(8,128)}, f32[4,2,24,384]{3,2,1,0:T(8,128)}, u32[]{:S(2)}, u32[]{:S(2)}) %collective-permute-start.25) | collective-permute-done | bytes 294944 | tf_op jit(solution)/shard_map/ppermute | solution.py:525
  128.1 3.0 %collective-permute-start.11 = (f32[5,2688]{1,0:T(8,128)S(1)}, f32[5,2688]{1,0:T(8,128)S(1)}, u32[]{:S(2)}, u32[]{:S(2)}) collective-permute-start(f32[5,2688]{1,0:T(8,128)S(1)} %add.288), channel_id=1, source_target_pairs={{0,96},{2,98},{4,100},{6,102},{8,104},{10,106},{12,108},{14,110},{... | collective-permute-start | bytes 161288 | tf_op jit(solution)/shard_map/ppermute | solution.py:525
  131.8 1.6 collective-permute-start.9
  133.3 1.3 fusion.17
  134.7 1.7 collective-permute-start.28
  136.4 4.5 %fusion.6 = f32[768,1024]{1,0:T(8,128)S(1)} fusion(f32[768,1024]{1,0:T(8,128)} %collective-permute-done.12, bf16[1024,768]{1,0:T(8,128)(2,1)S(1)} %copy-done.6, s32[]{:T(128)S(6)} %select_n.190, bf16[1024,1920]{1,0:T(8,128)(2,1)} %get-tuple-element.41), kind=kOutput, calls=%fused_computation.12 | convolution fusion | flops 1611399168 | bytes 11796484 | tf_op jit(solution)/shard_map/dot_general | solution.py:30
  140.9 2.1 collective-permute-start.27
  144.0 2.6 collective-permute-start.15
  147.0 1.9 collective-permute-start.14
  148.9 1.1 collective-permute-start.13
  153.0 26.3 %collective-permute-done.15 = f32[2,4,24,1024]{3,2,1,0:T(8,128)S(1)} collective-permute-done((f32[2,4,24,1024]{3,2,1,0:T(8,128)S(1)}, f32[2,4,24,1024]{3,2,1,0:T(8,128)S(1)}, u32[]{:S(2)}, u32[]{:S(2)}) %collective-permute-start.15) | collective-permute-done | bytes 786464 | tf_op jit(solution)/shard_map/ppermute | solution.py:525
  179.3 3.6 %collective-permute-start.29 = (f32[24,384]{1,0:T(8,128)S(1)}, f32[24,384]{1,0:T(8,128)S(1)}, u32[]{:S(2)}, u32[]{:S(2)}) collective-permute-start(f32[24,384]{1,0:T(8,128)S(1)} %dynamic-slice_bitcast_fusion.13), channel_id=1, source_target_pairs={{0,16},{2,18},{4,20},{6,22},{8,24},{10,26},{12,28},{14,30},{16,0},... | collective-permute-start | bytes 110600 | tf_op jit(solution)/shard_map/ppermute | solution.py:525
  183.3 2.1 collective-permute-start.18
  186.0 75.5 %collective-permute-done.29 = f32[24,384]{1,0:T(8,128)S(1)} collective-permute-done((f32[24,384]{1,0:T(8,128)S(1)}, f32[24,384]{1,0:T(8,128)S(1)}, u32[]{:S(2)}, u32[]{:S(2)}) %collective-permute-start.29) | collective-permute-done | bytes 36896 | tf_op jit(solution)/shard_map/ppermute | solution.py:525
  261.4 1.4 collective-permute-start.16
  263.0 5.3 %collective-permute-done.16 = f32[2,24,1024]{2,1,0:T(8,128)S(1)} collective-permute-done((f32[2,24,1024]{2,1,0:T(8,128)S(1)}, f32[2,24,1024]{2,1,0:T(8,128)S(1)}, u32[]{:S(2)}, u32[]{:S(2)}) %collective-permute-start.16) | collective-permute-done | bytes 196640 | tf_op jit(solution)/shard_map/ppermute | solution.py:525
  268.4 1.1 collective-permute-start.19
  270.1 4.5 %collective-permute-done.19 = f32[24,1024]{1,0:T(8,128)S(1)} collective-permute-done((f32[24,1024]{1,0:T(8,128)S(1)}, f32[24,1024]{1,0:T(8,128)S(1)}, u32[]{:S(2)}, u32[]{:S(2)}) %collective-permute-start.19) | collective-permute-done | bytes 98336 | tf_op jit(solution)/shard_map/ppermute | solution.py:525
  274.8 1.8 fusion.7
  276.6 1.1 collective-permute-start.21
  277.7 1.7 fusion.8
  (137 shorter events, 17.9 us)
Async XLA Ops:
  8.0 8.0 %copy-start.13 = (f32[4,768]{1,0:T(4,128)S(1)}, f32[4,768]{1,0:T(4,128)}, u32[]{:S(2)}) copy-start(f32[4,768]{1,0:T(4,128)} %param.24) | copy-start | bytes 36868
  8.0 8.0 %copy-start.21 = (f32[12]{0:T(128)S(1)}, f32[12]{0:T(128)}, u32[]{:S(2)}) copy-start(f32[12]{0:T(128)} %param.29) | copy-start | bytes 148
  8.0 8.0 %copy-start.19 = (f32[12]{0:T(128)S(1)}, f32[12]{0:T(128)}, u32[]{:S(2)}) copy-start(f32[12]{0:T(128)} %param.30) | copy-start | bytes 148
  8.0 8.7 %copy-start.17 = (bf16[768]{0:T(1024)(128)(2,1)S(1)}, bf16[768]{0:T(1024)(128)(2,1)}, u32[]{:S(2)}) copy-start(bf16[768]{0:T(1024)(128)(2,1)} %param.31) | copy-start | bytes 4612
  18.1 2.8 copy-start.20
  18.1 3.3 %copy-start.8 = (bf16[768,256]{1,0:T(8,128)(2,1)S(1)}, bf16[768,256]{1,0:T(8,128)(2,1)}, u32[]{:S(2)}) copy-start(bf16[768,256]{1,0:T(8,128)(2,1)} %param.22) | copy-start | bytes 1179652
  20.3 2.8 copy-start.14
  46.9 3.7 %collective-permute-start = (f32[2,1024]{1,0:T(2,128)S(1)}, f32[2,1024]{1,0:T(2,128)S(1)}, u32[]{:S(2)}, u32[]{:S(2)}) collective-permute-start(f32[2,1024]{1,0:T(2,128)S(1)} %slice.109), channel_id=1, source_target_pairs={{0,1},{1,0},{2,3},{3,2},{4,5},{5,4},{6,7},{7,6},{8,9},{9,8},{10,11... | collective-permute-start | bytes 24584 | tf_op jit(solution)/shard_map/ppermute | solution.py:428
  52.0 40.7 %copy-start.5 = (bf16[1024,768]{1,0:T(8,128)(2,1)S(1)}, bf16[1024,768]{1,0:T(8,128)(2,1)}, u32[]{:S(2)}) copy-start(bf16[1024,768]{1,0:T(8,128)(2,1)} %get-tuple-element.40) | copy-start | bytes 4718596
  90.6 9.9 %collective-permute-start.3 = (f32[8,1024]{1,0:T(8,128)S(1)}, f32[8,1024]{1,0:T(8,128)S(1)}, u32[]{:S(2)}, u32[]{:S(2)}) collective-permute-start(f32[8,1024]{1,0:T(8,128)S(1)} %pad_maximum_fusion.3), channel_id=1, source_target_pairs={{0,1},{1,0},{2,3},{3,2},{4,5},{5,4},{6,7},{7,6},{8,9},{9,8},{10,11... | collective-permute-start | bytes 98312 | tf_op jit(solution)/shard_map/ppermute | solution.py:483
  92.6 5.1 %copy-start.2 = (bf16[1,1024,768]{2,1,0:T(8,128)(2,1)S(1)}, bf16[1,1024,768]{2,1,0:T(8,128)(2,1)}, u32[]{:S(2)}) copy-start(bf16[1,1024,768]{2,1,0:T(8,128)(2,1)} %param.33) | copy-start | bytes 4718596
  92.6 5.1 %copy-start.22 = (bf16[1024,768]{1,0:T(8,128)(2,1)S(1)}, bf16[1024,768]{1,0:T(8,128)(2,1)}, u32[]{:S(2)}) copy-start(bf16[1024,768]{1,0:T(8,128)(2,1)} %get-tuple-element.42) | copy-start | bytes 4718596
  97.8 36.9 %collective-permute-start.12 = (f32[768,1024]{1,0:T(8,128)}, f32[768,1024]{1,0:T(8,128)}, u32[]{:S(2)}, u32[]{:S(2)}) collective-permute-start(f32[768,1024]{1,0:T(8,128)} %fusion.5), channel_id=1, source_target_pairs={{0,2},{2,0},{4,6},{6,4},{8,10},{10,8},{12,14},{14,12},{16,18},{18,... | collective-permute-start | bytes 9437192 | tf_op jit(solution)/shard_map/ppermute | solution.py:525
  97.8 2.7 copy-start.10
  97.8 2.7 copy-start.12
  100.0 8.2 %collective-permute-start.22 = (f32[768,384]{1,0:T(8,128)}, f32[768,384]{1,0:T(8,128)}, u32[]{:S(2)}, u32[]{:S(2)}) collective-permute-start(f32[768,384]{1,0:T(8,128)} %fusion.11), channel_id=1, source_target_pairs={{0,2},{2,0},{4,6},{6,4},{8,10},{10,8},{12,14},{14,12},{16,18},{18,... | collective-permute-start | bytes 3538952 | tf_op jit(solution)/shard_map/ppermute | solution.py:525
  100.6 3.1 %collective-permute-start.4 = (f32[5,2688]{1,0:T(8,128)S(1)}, f32[5,2688]{1,0:T(8,128)S(1)}, u32[]{:S(2)}, u32[]{:S(2)}) collective-permute-start(f32[5,2688]{1,0:T(8,128)S(1)} %pad_maximum_fusion), channel_id=1, source_target_pairs={{0,2},{2,0},{4,6},{6,4},{8,10},{10,8},{12,14},{14,12},{16,18},{18,... | collective-permute-start | bytes 161288 | tf_op jit(solution)/shard_map/ppermute | solution.py:525
  103.7 20.0 %copy-start = (f32[1024,768]{1,0:T(8,128)S(1)}, f32[1024,768]{1,0:T(8,128)}, u32[]{:S(2)}) copy-start(f32[1024,768]{1,0:T(8,128)} %get-tuple-element.30) | copy-start | bytes 9437188
  103.7 11.9 %collective-permute-start.7 = (f32[5,2688]{1,0:T(8,128)S(1)}, f32[5,2688]{1,0:T(8,128)S(1)}, u32[]{:S(2)}, u32[]{:S(2)}) collective-permute-start(f32[5,2688]{1,0:T(8,128)S(1)} %fusion.46), channel_id=1, source_target_pairs={{0,12},{2,14},{4,0},{6,2},{8,4},{10,6},{12,8},{14,10},{16,28},{18,... | collective-permute-start | bytes 161288 | tf_op jit(solution)/shard_map/ppermute | solution.py:525
  106.5 10.6 %collective-permute-start.6 = (f32[5,2688]{1,0:T(8,128)S(1)}, f32[5,2688]{1,0:T(8,128)S(1)}, u32[]{:S(2)}, u32[]{:S(2)}) collective-permute-start(f32[5,2688]{1,0:T(8,128)S(1)} %fusion.46), channel_id=1, source_target_pairs={{0,8},{2,10},{4,12},{6,14},{8,0},{10,2},{12,4},{14,6},{16,24},{18,... | collective-permute-start | bytes 161288 | tf_op jit(solution)/shard_map/ppermute | solution.py:525
  107.4 9.8 %collective-permute-start.5 = (f32[5,2688]{1,0:T(8,128)S(1)}, f32[5,2688]{1,0:T(8,128)S(1)}, u32[]{:S(2)}, u32[]{:S(2)}) collective-permute-start(f32[5,2688]{1,0:T(8,128)S(1)} %fusion.46), channel_id=1, source_target_pairs={{0,4},{2,6},{4,8},{6,10},{8,12},{10,14},{12,0},{14,2},{16,20},{18,... | collective-permute-start | bytes 161288 | tf_op jit(solution)/shard_map/ppermute | solution.py:525
  113.3 14.8 %collective-permute-start.25 = (f32[4,2,24,384]{3,2,1,0:T(8,128)}, f32[4,2,24,384]{3,2,1,0:T(8,128)}, u32[]{:S(2)}, u32[]{:S(2)}) collective-permute-start(f32[4,2,24,384]{3,2,1,0:T(8,128)} %get-tuple-element.54), channel_id=1, source_target_pairs={{0,12},{2,14},{4,0},{6,2},{8,4},{10,6},{12,8},{14,10},{16,28},{18,... | collective-permute-start | bytes 884744 | tf_op jit(solution)/shard_map/ppermute | solution.py:525
  115.6 15.5 %collective-permute-start.24 = (f32[4,2,24,384]{3,2,1,0:T(8,128)}, f32[4,2,24,384]{3,2,1,0:T(8,128)}, u32[]{:S(2)}, u32[]{:S(2)}) collective-permute-start(f32[4,2,24,384]{3,2,1,0:T(8,128)} %get-tuple-element.55), channel_id=1, source_target_pairs={{0,8},{2,10},{4,12},{6,14},{8,0},{10,2},{12,4},{14,6},{16,24},{18,... | collective-permute-start | bytes 884744 | tf_op jit(solution)/shard_map/ppermute | solution.py:525
  117.1 14.6 %collective-permute-start.23 = (f32[4,2,24,384]{3,2,1,0:T(8,128)S(1)}, f32[4,2,24,384]{3,2,1,0:T(8,128)}, u32[]{:S(2)}, u32[]{:S(2)}) collective-permute-start(f32[4,2,24,384]{3,2,1,0:T(8,128)S(1)} %get-tuple-element.53), channel_id=1, source_target_pairs={{0,4},{2,6},{4,8},{6,10},{8,12},{10,14},{12,0},{14,2},{16,20},{18,... | collective-permute-start | bytes 884744 | tf_op jit(solution)/shard_map/ppermute | solution.py:525
  117.2 6.5 %collective-permute-start.8 = (f32[5,2688]{1,0:T(8,128)S(1)}, f32[5,2688]{1,0:T(8,128)}, u32[]{:S(2)}, u32[]{:S(2)}) collective-permute-start(f32[5,2688]{1,0:T(8,128)S(1)} %add_add_fusion.1), channel_id=1, source_target_pairs={{0,16},{2,18},{4,20},{6,22},{8,24},{10,26},{12,28},{14,30},{16,0},... | collective-permute-start | bytes 161288 | tf_op jit(solution)/shard_map/ppermute | solution.py:525
  120.8 15.6 %copy-start.6 = (bf16[1024,768]{1,0:T(8,128)(2,1)S(1)}, bf16[1024,768]{1,0:T(8,128)(2,1)}, u32[]{:S(2)}) copy-start(bf16[1024,768]{1,0:T(8,128)(2,1)} %get-tuple-element.40) | copy-start | bytes 4718596
  123.7 151.0 %collective-permute-start.1 = (f32[1024,768]{1,0:T(8,128)S(1)}, f32[1024,768]{1,0:T(8,128)S(1)}, u32[]{:S(2)}, u32[]{:S(2)}) collective-permute-start(f32[1024,768]{1,0:T(8,128)S(1)} %copy-done), channel_id=1, source_target_pairs={{0,1},{1,0},{2,3},{3,2},{4,5},{5,4},{6,7},{7,6},{8,9},{9,8},{10,11... | collective-permute-start | bytes 9437192 | tf_op jit(solution)/shard_map/ppermute | solution.py:432
  128.1 12.8 %collective-permute-start.11 = (f32[5,2688]{1,0:T(8,128)S(1)}, f32[5,2688]{1,0:T(8,128)S(1)}, u32[]{:S(2)}, u32[]{:S(2)}) collective-permute-start(f32[5,2688]{1,0:T(8,128)S(1)} %add.288), channel_id=1, source_target_pairs={{0,96},{2,98},{4,100},{6,102},{8,104},{10,106},{12,108},{14,110},{... | collective-permute-start | bytes 161288 | tf_op jit(solution)/shard_map/ppermute | solution.py:525
  131.1 11.9 %collective-permute-start.10 = (f32[5,2688]{1,0:T(8,128)S(1)}, f32[5,2688]{1,0:T(8,128)S(1)}, u32[]{:S(2)}, u32[]{:S(2)}) collective-permute-start(f32[5,2688]{1,0:T(8,128)S(1)} %add.288), channel_id=1, source_target_pairs={{0,64},{2,66},{4,68},{6,70},{8,72},{10,74},{12,76},{14,78},{16,80}... | collective-permute-start | bytes 161288 | tf_op jit(solution)/shard_map/ppermute | solution.py:525
  131.8 12.1 %collective-permute-start.9 = (f32[5,2688]{1,0:T(8,128)S(1)}, f32[5,2688]{1,0:T(8,128)S(1)}, u32[]{:S(2)}, u32[]{:S(2)}) collective-permute-start(f32[5,2688]{1,0:T(8,128)S(1)} %add.288), channel_id=1, source_target_pairs={{0,32},{2,34},{4,36},{6,38},{8,40},{10,42},{12,44},{14,46},{16,48}... | collective-permute-start | bytes 161288 | tf_op jit(solution)/shard_map/ppermute | solution.py:525
  134.7 9.4 %collective-permute-start.28 = (f32[2,24,384]{2,1,0:T(8,128)S(1)}, f32[2,24,384]{2,1,0:T(8,128)S(1)}, u32[]{:S(2)}, u32[]{:S(2)}) collective-permute-start(f32[2,24,384]{2,1,0:T(8,128)S(1)} %get-tuple-element.60), channel_id=1, source_target_pairs={{0,96},{2,98},{4,100},{6,102},{8,104},{10,106},{12,108},{14,110},{... | collective-permute-start | bytes 221192 | tf_op jit(solution)/shard_map/ppermute | solution.py:525
  140.9 3.0 %copy-start.1 = (f32[1024,768]{1,0:T(8,128)S(1)}, f32[1024,768]{1,0:T(8,128)}, u32[]{:S(2)}) copy-start(f32[1024,768]{1,0:T(8,128)} %get-tuple-element.35) | copy-start | bytes 9437188
  140.9 6.1 %collective-permute-start.27 = (f32[2,24,384]{2,1,0:T(8,128)S(1)}, f32[2,24,384]{2,1,0:T(8,128)S(1)}, u32[]{:S(2)}, u32[]{:S(2)}) collective-permute-start(f32[2,24,384]{2,1,0:T(8,128)S(1)} %get-tuple-element.61), channel_id=1, source_target_pairs={{0,64},{2,66},{4,68},{6,70},{8,72},{10,74},{12,76},{14,78},{16,80}... | collective-permute-start | bytes 221192 | tf_op jit(solution)/shard_map/ppermute | solution.py:525
  143.0 5.9 %collective-permute-start.26 = (f32[2,24,384]{2,1,0:T(8,128)S(1)}, f32[2,24,384]{2,1,0:T(8,128)S(1)}, u32[]{:S(2)}, u32[]{:S(2)}) collective-permute-start(f32[2,24,384]{2,1,0:T(8,128)S(1)} %get-tuple-element.59), channel_id=1, source_target_pairs={{0,32},{2,34},{4,36},{6,38},{8,40},{10,42},{12,44},{14,46},{16,48}... | collective-permute-start | bytes 221192 | tf_op jit(solution)/shard_map/ppermute | solution.py:525
  143.9 133.8 %collective-permute-start.2 = (f32[1024,768]{1,0:T(8,128)S(1)}, f32[1024,768]{1,0:T(8,128)S(1)}, u32[]{:S(2)}, u32[]{:S(2)}) collective-permute-start(f32[1024,768]{1,0:T(8,128)S(1)} %copy-done.1), channel_id=1, source_target_pairs={{0,1},{1,0},{2,3},{3,2},{4,5},{5,4},{6,7},{7,6},{8,9},{9,8},{10,11... | collective-permute-start | bytes 9437192 | tf_op jit(solution)/shard_map/ppermute | solution.py:473
  144.0 35.2 %collective-permute-start.15 = (f32[2,4,24,1024]{3,2,1,0:T(8,128)S(1)}, f32[2,4,24,1024]{3,2,1,0:T(8,128)S(1)}, u32[]{:S(2)}, u32[]{:S(2)}) collective-permute-start(f32[2,4,24,1024]{3,2,1,0:T(8,128)S(1)} %get-tuple-element.49), channel_id=1, source_target_pairs={{0,96},{2,98},{4,100},{6,102},{8,104},{10,106},{12,108},{14,110},{... | collective-permute-start | bytes 2359304 | tf_op jit(solution)/shard_map/ppermute | solution.py:525
  147.0 35.9 %collective-permute-start.14 = (f32[2,4,24,1024]{3,2,1,0:T(8,128)S(1)}, f32[2,4,24,1024]{3,2,1,0:T(8,128)S(1)}, u32[]{:S(2)}, u32[]{:S(2)}) collective-permute-start(f32[2,4,24,1024]{3,2,1,0:T(8,128)S(1)} %get-tuple-element.50), channel_id=1, source_target_pairs={{0,64},{2,66},{4,68},{6,70},{8,72},{10,74},{12,76},{14,78},{16,80}... | collective-permute-start | bytes 2359304 | tf_op jit(solution)/shard_map/ppermute | solution.py:525
  148.9 34.0 %collective-permute-start.13 = (f32[2,4,24,1024]{3,2,1,0:T(8,128)S(1)}, f32[2,4,24,1024]{3,2,1,0:T(8,128)S(1)}, u32[]{:S(2)}, u32[]{:S(2)}) collective-permute-start(f32[2,4,24,1024]{3,2,1,0:T(8,128)S(1)} %get-tuple-element.48), channel_id=1, source_target_pairs={{0,32},{2,34},{4,36},{6,38},{8,40},{10,42},{12,44},{14,46},{16,48}... | collective-permute-start | bytes 2359304 | tf_op jit(solution)/shard_map/ppermute | solution.py:525
  153.0 121.8 %copy-start.4 = (bf16[1,1024,768]{2,1,0:T(8,128)(2,1)S(1)}, bf16[1,1024,768]{2,1,0:T(8,128)(2,1)}, u32[]{:S(2)}) copy-start(bf16[1,1024,768]{2,1,0:T(8,128)(2,1)} %param.18) | copy-start | bytes 4718596
  179.3 82.1 %collective-permute-start.29 = (f32[24,384]{1,0:T(8,128)S(1)}, f32[24,384]{1,0:T(8,128)S(1)}, u32[]{:S(2)}, u32[]{:S(2)}) collective-permute-start(f32[24,384]{1,0:T(8,128)S(1)} %dynamic-slice_bitcast_fusion.13), channel_id=1, source_target_pairs={{0,16},{2,18},{4,20},{6,22},{8,24},{10,26},{12,28},{14,30},{16,0},... | collective-permute-start | bytes 110600 | tf_op jit(solution)/shard_map/ppermute | solution.py:525
  183.3 79.6 %collective-permute-start.18 = (f32[2,24,1024]{2,1,0:T(8,128)S(1)}, f32[2,24,1024]{2,1,0:T(8,128)S(1)}, u32[]{:S(2)}, u32[]{:S(2)}) collective-permute-start(f32[2,24,1024]{2,1,0:T(8,128)S(1)} %get-tuple-element.57), channel_id=1, source_target_pairs={{0,12},{2,14},{4,0},{6,2},{8,4},{10,6},{12,8},{14,10},{16,28},{18,... | collective-permute-start | bytes 589832 | tf_op jit(solution)/shard_map/ppermute | solution.py:525
  185.4 77.6 %collective-permute-start.17 = (f32[2,24,1024]{2,1,0:T(8,128)S(1)}, f32[2,24,1024]{2,1,0:T(8,128)S(1)}, u32[]{:S(2)}, u32[]{:S(2)}) collective-permute-start(f32[2,24,1024]{2,1,0:T(8,128)S(1)} %get-tuple-element.58), channel_id=1, source_target_pairs={{0,8},{2,10},{4,12},{6,14},{8,0},{10,2},{12,4},{14,6},{16,24},{18,... | collective-permute-start | bytes 589832 | tf_op jit(solution)/shard_map/ppermute | solution.py:525
  261.4 6.9 %collective-permute-start.16 = (f32[2,24,1024]{2,1,0:T(8,128)S(1)}, f32[2,24,1024]{2,1,0:T(8,128)S(1)}, u32[]{:S(2)}, u32[]{:S(2)}) collective-permute-start(f32[2,24,1024]{2,1,0:T(8,128)S(1)} %get-tuple-element.56), channel_id=1, source_target_pairs={{0,4},{2,6},{4,8},{6,10},{8,12},{10,14},{12,0},{14,2},{16,20},{18,... | collective-permute-start | bytes 589832 | tf_op jit(solution)/shard_map/ppermute | solution.py:525
  262.9 6.6 %collective-permute-start.30 = (f32[12,384]{1,0:T(8,128)S(1)}, f32[12,384]{1,0:T(8,128)S(1)}, u32[]{:S(2)}, u32[]{:S(2)}) collective-permute-start(f32[12,384]{1,0:T(8,128)S(1)} %get-tuple-element.68), channel_id=1, source_target_pairs={{0,2},{2,0},{4,6},{6,4},{8,10},{10,8},{12,14},{14,12},{16,18},{18,... | collective-permute-start | bytes 55304 | tf_op jit(solution)/shard_map/ppermute | solution.py:525
  268.4 6.2 %collective-permute-start.19 = (f32[24,1024]{1,0:T(8,128)S(1)}, f32[24,1024]{1,0:T(8,128)S(1)}, u32[]{:S(2)}, u32[]{:S(2)}) collective-permute-start(f32[24,1024]{1,0:T(8,128)S(1)} %dynamic-slice_bitcast_fusion.9), channel_id=1, source_target_pairs={{0,16},{2,18},{4,20},{6,22},{8,24},{10,26},{12,28},{14,30},{16,0},... | collective-permute-start | bytes 294920 | tf_op jit(solution)/shard_map/ppermute | solution.py:525
  274.6 3.0 %copy-start.3 = (bf16[1,1024,768]{2,1,0:T(8,128)(2,1)S(1)}, bf16[1,1024,768]{2,1,0:T(8,128)(2,1)}, u32[]{:S(2)}) copy-start(bf16[1,1024,768]{2,1,0:T(8,128)(2,1)} %param.33) | copy-start | bytes 4718596
  274.6 1.9 collective-permute-start.20
  276.6 4.1 %collective-permute-start.21 = (f32[12,256]{1,0:T(8,128)S(1)}, f32[12,256]{1,0:T(8,128)S(1)}, u32[]{:S(2)}, u32[]{:S(2)}) collective-permute-start(f32[12,256]{1,0:T(8,128)S(1)} %slice.133), channel_id=1, source_target_pairs={{0,1},{1,0},{2,3},{3,2},{4,5},{5,4},{6,7},{7,6},{8,9},{9,8},{10,11... | collective-permute-start | bytes 36872 | tf_op jit(solution)/shard_map/ppermute | solution.py:479
  (6 other events, 12.4 us)
